TPU v7x, 32 devices: a whole 2x2x4 slice. The times are simulated.
32 devices in a mesh: dp: 8 (over z, y), tensor: 4 (over x, core).
Axes of the slice: x: 2, y: 2, z: 4, core: 2. Of those that a mesh axis runs over, the one named last changes fastest.
Arguments:
- tokens: bfloat16 [1024, 3072], P('dp', 'tensor'), may hold values from -6 to 6
- grad_out: bfloat16 [1024, 3072], P('dp', 'tensor'), may hold values from -6 to 6
- expert_ids: int32 [1024, 2], P('dp'), may hold values from 0 to 7, as said below
- gate_probs: float32 [1024, 2], P('dp'), may hold values from 0.2 to 1
- w_gate: bfloat16 [8, 3072, 8192], P('dp', None, 'tensor'), may hold values from -0.109375 to 0.109375
- w_up: bfloat16 [8, 3072, 8192], P('dp', None, 'tensor'), may hold values from -0.109375 to 0.109375
- w_down: bfloat16 [8, 8192, 3072], P('dp', 'tensor'), may hold values from -0.0625 to 0.0625
Outputs:
- input_grad: bfloat16 [1024, 3072], P('dp', 'tensor')
- grad_gate: bfloat16 [8, 3072, 8192], P('dp', None, 'tensor')
- grad_up: bfloat16 [8, 3072, 8192], P('dp', None, 'tensor')
- grad_down: bfloat16 [8, 8192, 3072], P('dp', 'tensor')
Inputs may be any that keep to these rules, and one draw needn't show every extreme that they name: `expert_ids`: A token's two experts differ. Among the 128 tokens of one index of dp (aligned blocks of rows), no expert is named more than 33 times, and one expert, the same in every block, is named exactly 33 times in each block.
All inputs are finite; a program needn't handle non-finite values.
Results may differ from a plain program's by a relative error of at most 0.015.
Values may be sent and summed in bfloat16 or wider, within the bound.
No kernel may reach another device: no remote copies, remote signals or barrier semaphores. Data moves between devices by JAX's collectives and lax.ppermute only.
A program may use at most 192 MiB of HBM per device.

v0:
```python
import jax
import jax.numpy as jnp
from jax import lax
from jax.sharding import PartitionSpec as P

EXPERTS = 8
TOP = 2
CAP = 33


def contract_last(left, right):
    return lax.dot_general(
        left, right, (((1,), (1,)), ((), ())), preferred_element_type=jnp.float32
    )


def contract_first(left, right):
    return lax.dot_general(
        left, right, (((0,), (0,)), ((), ())), preferred_element_type=jnp.float32
    )


def expert_work(expert_rows, expert_grads, gate_shard, up_shard, down_shard):
    width = gate_shard.shape[1]
    paired_weights = jnp.concatenate([gate_shard, up_shard], axis=1)
    paired_value = jnp.dot(expert_rows, paired_weights, preferred_element_type=jnp.float32)
    gate_value = paired_value[:, :width]
    up_value = paired_value[:, width:]
    sigmoid_value = jax.nn.sigmoid(gate_value)
    silu_value = gate_value * sigmoid_value
    hidden = (silu_value * up_value).astype(jnp.bfloat16)
    hidden_grad = contract_last(expert_grads, down_shard)
    gate_grad = (
        hidden_grad * up_value * sigmoid_value * (1.0 + gate_value * (1.0 - sigmoid_value))
    ).astype(jnp.bfloat16)
    up_grad = (hidden_grad * silu_value).astype(jnp.bfloat16)
    paired_grad = jnp.concatenate([gate_grad, up_grad], axis=1)
    row_part = contract_last(paired_grad, paired_weights).astype(jnp.bfloat16)
    paired_total = contract_first(expert_rows, paired_grad)
    gate_total = paired_total[:, :width].astype(jnp.bfloat16)
    up_total = paired_total[:, width:].astype(jnp.bfloat16)
    down_total = contract_first(hidden, expert_grads).astype(jnp.bfloat16)
    return (row_part, gate_total, up_total, down_total)


def shards(tokens, grad_out, expert_ids, gate_probs, w_gate, w_up, w_down):
    dp_size = lax.axis_size("dp")
    slices = dp_size // EXPERTS
    token_count = tokens.shape[0]
    pair_count = token_count * TOP
    flat_ids = expert_ids.reshape(-1)
    experts_row = jnp.arange(EXPERTS, dtype=jnp.int32)
    onehot = (flat_ids[:, None] == experts_row[None, :]).astype(jnp.int32)
    slot_index = jnp.sum((jnp.cumsum(onehot, axis=0) - onehot) * onehot, axis=1)
    positions = jnp.arange(CAP, dtype=jnp.int32)
    matches = (flat_ids[None, None, :] == experts_row[:, None, None]) & (
        slot_index[None, None, :] == positions[None, :, None]
    )
    assignment = jnp.arange(pair_count, dtype=jnp.int32)
    lookup = jnp.sum(jnp.where(matches, assignment[None, None, :], 0), axis=2)
    lookup = lookup + jnp.where(jnp.any(matches, axis=2), 0, pair_count)
    owners = jnp.arange(dp_size, dtype=jnp.int32) // slices
    send_pairs = lookup[owners]
    send_tokens = jnp.where(send_pairs < pair_count, send_pairs // TOP, token_count)
    slice_row = jnp.arange(slices, dtype=jnp.int32)
    back_index = (flat_ids[:, None] * slices + slice_row[None, :]) * CAP + slot_index[:, None]
    gate_shard = w_gate[0]
    up_shard = w_up[0]
    down_shard = w_down[0]

    def padded(rows_in):
        return jnp.concatenate([rows_in, jnp.zeros((1, rows_in.shape[1]), rows_in.dtype)], axis=0)

    sent_rows = padded(tokens)[send_tokens]
    product = gate_probs[:, :, None] * grad_out[:, None, :].astype(jnp.float32)
    sent_grads = padded(product.astype(jnp.bfloat16).reshape(pair_count, grad_out.shape[1]))[
        send_pairs
    ]
    got_rows, got_grads = (
        lax.all_to_all(sent_rows, "dp", split_axis=0, concat_axis=0, tiled=True),
        lax.all_to_all(sent_grads, "dp", split_axis=0, concat_axis=0, tiled=True),
    )
    narrow = got_rows.shape[2]
    full_rows, full_grads = (
        lax.all_gather(got_rows.reshape(dp_size * CAP, narrow), "tensor", axis=1, tiled=True),
        lax.all_gather(got_grads.reshape(dp_size * CAP, narrow), "tensor", axis=1, tiled=True),
    )
    row_part, gate_total, up_total, down_total = expert_work(
        full_rows, full_grads, gate_shard, up_shard, down_shard
    )
    partial_value = lax.optimization_barrier(row_part).astype(jnp.float32)
    summed = lax.psum_scatter(
        partial_value.astype(jnp.bfloat16), "tensor", scatter_dimension=1, tiled=True
    ).astype(jnp.float32)
    returned = lax.all_to_all(
        summed.reshape(dp_size, CAP, narrow).astype(jnp.bfloat16),
        "dp",
        split_axis=0,
        concat_axis=0,
        tiled=True,
    ).astype(jnp.float32)
    flat_back = returned.reshape(dp_size * CAP, returned.shape[2])
    picked = flat_back[back_index].reshape(token_count, TOP * slices, returned.shape[2])
    input_grad = jnp.sum(picked, axis=1, dtype=jnp.float32)
    return (input_grad.astype(jnp.bfloat16), gate_total[None], up_total[None], down_total[None])


def solution(mesh):
    placed = (
        P("dp", "tensor"),
        P("dp", "tensor"),
        P("dp", None),
        P("dp", None),
        P("dp", None, "tensor"),
        P("dp", None, "tensor"),
        P("dp", "tensor", None),
    )
    return jax.shard_map(
        shards,
        mesh=mesh,
        in_specs=placed,
        out_specs=(
            P("dp", "tensor"),
            P("dp", None, "tensor"),
            P("dp", None, "tensor"),
            P("dp", "tensor", None),
        ),
        check_vma=False,
    )
```

profile of v0, /device:TPU:0, one launch (start us, length us, event | category | flops | bytes accessed | tf_op | source)
XLA Modules:
  0.0 170.4 jit_solution(16369439997218941189)
XLA Ops:
  7.2 0.0 all-gather.5.cloned.1.call-start
  7.2 0.8 copy.16
  8.0 0.1 eq.68
  8.1 0.1 eq.61
  8.3 0.6 reduce-window.6
  8.9 0.2 slice_reduce_fusion
  9.1 0.1 fusion.9
  9.3 0.7 fusion.6
  9.9 0.7 and_reduce_fusion
  10.6 0.1 copy.19
  10.6 0.1 copy.18
  10.8 0.6 gather_fusion
  11.3 0.1 reshape.235
  11.4 0.9 concatenate.13
  12.4 2.1 %gather_fusion.2 = bf16[264,768]{1,0:T(8,128)(2,1)S(1)} fusion(bf16[129,768]{1,0:T(8,128)(2,1)S(1)} %concatenate.13, s32[1024]{0:T(1024)S(1)} %pad_clamp_fusion.1), kind=kCustom, calls=%fused_computation.2 | custom fusion | bytes 812064 | tf_op jit(solution)/shard_map/gather | solution.py:74
  14.5 0.0 copy-start
  14.5 0.1 reshape.234
  14.6 20.9 %all_to_all.15 = bf16[8,33,768]{2,1,0:T(8,128)(2,1)S(1)} all-to-all(bf16[8,33,768]{2,1,0:T(8,128)(2,1)S(1)} %reshape.234), channel_id=1, replica_groups=mesh['dp'=8,'tensor'=4] {'dp'}, dimensions={0} | all-to-all | bytes 811008 | tf_op jit(solution)/shard_map/all_to_all | solution.py:80
  35.5 0.0 copy-start.2
  35.5 0.9 reshape.211
  36.4 0.0 all-gather.5.cloned.1.call-update
  36.5 0.0 copy-done
  36.5 0.2 mul.62
  36.7 0.5 mul.63
  37.2 0.0 copy-done.2
  37.2 0.1 copy.15
  37.3 0.1 mul.60
  37.5 0.1 multiply_convert_fusion.4
  37.6 0.1 reshape.227
  37.7 0.0 copy-start.1
  37.7 2.1 %gather_fusion.1 = bf16[264,768]{1,0:T(8,128)(2,1)S(1)} fusion(bf16[257,768]{1,0:T(8,128)(2,1)S(1)} %concatenate.12, s32[1024]{0:T(1024)S(1)} %pad_clamp_fusion.2), kind=kCustom, calls=%fused_computation.1 | custom fusion | bytes 812064 | tf_op jit(solution)/shard_map/gather | solution.py:76
  39.8 0.9 reshape.226
  40.8 3.6 %all-to-all-start = ((bf16[8,33,768]{2,1,0:T(8,128)(2,1)}), bf16[8,33,768]{2,1,0:T(8,128)(2,1)S(1)}, u32[]{:S(2)}, u32[]{:S(2)}) async-start(bf16[8,33,768]{2,1,0:T(8,128)(2,1)} %reshape.226), calls=%async_computation | async-start | bytes 983040 | tf_op jit(solution)/shard_map/all_to_all | solution.py:81
  44.3 0.0 all-gather.3.cloned.1.call-start
  44.4 0.0 copy-done.1
  44.4 0.1 copy.20
  44.5 0.1 mul.74
  44.7 13.2 %all-to-all-done = bf16[8,33,768]{2,1,0:T(8,128)(2,1)S(1)} async-done(((bf16[8,33,768]{2,1,0:T(8,128)(2,1)}), bf16[8,33,768]{2,1,0:T(8,128)(2,1)S(1)}, u32[]{:S(2)}, u32[]{:S(2)}) %all-to-all-start) | async-done | bytes 405536 | tf_op jit(solution)/shard_map/all_to_all | solution.py:81
  57.9 0.9 reshape.210
  58.8 0.0 all-gather.3.cloned.1.call-update
  58.8 0.2 reduce-scatter.2.cloned.1.call-start
  59.0 0.0 all-gather.5.cloned.1.call-done
  59.0 14.4 %fusion.1 = f32[264,4096]{1,0:T(8,128)} fusion(bf16[264,3072]{1,0:T(8,128)(2,1)} %all-gather.5.cloned.1.call-done, bf16[3072,2048]{1,0:T(8,128)(2,1)} %bitcast.55, bf16[3072,2048]{1,0:T(8,128)(2,1)} %bitcast.57), kind=kOutput, calls=%fused_computation.7 | convolution fusion | flops 6694109184 | bytes 31113216 | tf_op jit(solution)/shard_map/dot_general | solution.py:26
  73.4 4.5 %all-gather.3.cloned.1.call-done = bf16[264,3072]{1,0:T(8,128)(2,1)} async-done(((bf16[264,768]{1,0:T(8,128)(2,1)}), bf16[264,3072]{1,0:T(8,128)(2,1)}) %all-gather.3.cloned.1.call-update) | async-done | bytes 1622032 | tf_op jit(solution)/shard_map/all_gather | solution.py:86
  77.9 10.3 %multiply_convert_fusion.2 = (bf16[264,2048]{1,0:T(8,128)(2,1)S(1)}, bf16[264,2048]{1,0:T(8,128)(2,1)S(1)}) fusion(f32[264,4096]{1,0:T(8,128)} %fusion.1, bf16[264,3072]{1,0:T(8,128)(2,1)} %all-gather.3.cloned.1.call-done, bf16[1,2048,3072]{2,1,0:T(8,128)(2,1)} %param.13), kind=kOutput, calls=%fused_computation.17 | convolution fusion | flops 3328917504 | bytes 20692992 | tf_op jit(solution)/shard_map/dot_general | solution.py:12
  88.2 0.0 copy-start.5
  88.2 1.0 copy-done.5
  89.2 0.0 copy-start.3
  89.2 13.1 %fusion.4 = bf16[264,3072]{1,0:T(8,128)(2,1)} fusion(bf16[3072,2048]{1,0:T(8,128)(2,1)} %bitcast.56, bf16[3072,2048]{1,0:T(8,128)(2,1)} %bitcast.58, bf16[264,2048]{1,0:T(8,128)(2,1)S(1)} %get-tuple-element.7, bf16[264,2048]{1,0:T(8,128)(2,1)S(1)} %get-tuple-element.6), kind=kOutput, calls=%fused_computation.13 | convolution fusion | flops 6699245568 | bytes 28950528 | tf_op jit(solution)/shard_map/dot_general | solution.py:12
  102.3 0.0 reduce-scatter.2.cloned.1.call-update
  102.3 0.0 copy-done.3
  102.3 18.5 %convolution_convert_fusion = bf16[3072,4096]{1,0:T(8,128)(2,1)} fusion(bf16[264,3072]{1,0:T(8,128)(2,1)S(1)} %copy-done.3, bf16[264,2048]{1,0:T(8,128)(2,1)} %copy-done.5, bf16[264,2048]{1,0:T(8,128)(2,1)S(1)} %get-tuple-element.6), kind=kOutput, calls=%fused_computation.5 | convolution fusion | flops 6660685824 | bytes 28950528 | tf_op jit(solution)/shard_map/dot_general | solution.py:18
  120.9 0.0 copy-start.4
  120.9 18.0 %slice_bitcast_fusion = (bf16[1,3072,2048]{2,1,0:T(8,128)(2,1)}, bf16[1,3072,2048]{2,1,0:T(8,128)(2,1)}) fusion(bf16[3072,4096]{1,0:T(8,128)(2,1)} %convolution_convert_fusion), kind=kLoop, calls=%fused_computation.8 | loop fusion | bytes 50331648 | tf_op jit(solution)/shard_map/broadcast_in_dim | solution.py:105
  138.9 0.0 reduce-scatter.2.cloned.1.call-done
  138.9 1.9 %convert_element_type.50 = bf16[8,33,768]{2,1,0:T(8,128)(2,1)} reshape(bf16[264,768]{1,0:T(8,128)(2,1)} %reduce-scatter.2.cloned.1.call-done) | data formatting | bytes 811008 | tf_op jit(solution)/shard_map/convert_element_type | solution.py:96
  140.8 5.5 %all-to-all-start.2 = ((bf16[8,33,768]{2,1,0:T(8,128)(2,1)}), bf16[8,33,768]{2,1,0:T(8,128)(2,1)S(1)}, u32[]{:S(2)}, u32[]{:S(2)}) async-start(bf16[8,33,768]{2,1,0:T(8,128)(2,1)} %convert_element_type.50), calls=%async_computation.3 | async-start | bytes 983040 | tf_op jit(solution)/shard_map/all_to_all | solution.py:95
  146.3 0.0 copy-done.4
  146.3 12.2 %convert_bitcast_fusion = bf16[1,2048,3072]{2,1,0:T(8,128)(2,1)} fusion(bf16[264,3072]{1,0:T(8,128)(2,1)S(1)} %copy-done.4, f32[264,4096]{1,0:T(8,128)} %fusion.1), kind=kOutput, calls=%fused_computation.12 | convolution fusion | flops 3331424256 | bytes 18530304 | tf_op jit(solution)/shard_map/dot_general | solution.py:18
  158.5 2.0 %all-to-all-done.2 = bf16[8,33,768]{2,1,0:T(8,128)(2,1)S(1)} async-done(((bf16[8,33,768]{2,1,0:T(8,128)(2,1)}), bf16[8,33,768]{2,1,0:T(8,128)(2,1)S(1)}, u32[]{:S(2)}, u32[]{:S(2)}) %all-to-all-start.2) | async-done | bytes 405536 | tf_op jit(solution)/shard_map/all_to_all | solution.py:95
  160.5 0.1 reshape.216
  160.6 1.1 gather_fusion.3
  161.7 0.5 reshape.214
  162.2 1.7 reduce_sum.32
  (15 shorter events, 0.2 us)
Async XLA Ops:
  7.2 51.9 %all-gather.5.cloned.1.call-start = ((), (), s32[]{:S(2)}) async-start(), calls=%async_computation.5 | async-start | bytes 2027520 | tf_op jit(solution)/shard_map/all_gather | solution.py:85
  14.5 22.0 %copy-start = (bf16[128,768]{1,0:T(8,128)(2,1)S(1)}, bf16[128,768]{1,0:T(8,128)(2,1)}, u32[]{:S(2)}) copy-start(bf16[128,768]{1,0:T(8,128)(2,1)} %param.8) | copy-start | bytes 589828
  35.5 1.7 copy-start.2
  37.7 6.7 %copy-start.1 = (s32[128,2]{0,1:T(2,128)S(1)}, s32[128,2]{0,1:T(2,128)}, u32[]{:S(2)}) copy-start(s32[128,2]{0,1:T(2,128)} %param.9) | copy-start | bytes 3076
  40.8 17.1 %all-to-all-start = ((bf16[8,33,768]{2,1,0:T(8,128)(2,1)}), bf16[8,33,768]{2,1,0:T(8,128)(2,1)S(1)}, u32[]{:S(2)}, u32[]{:S(2)}) async-start(bf16[8,33,768]{2,1,0:T(8,128)(2,1)} %reshape.226), calls=%async_computation | async-start | bytes 983040 | tf_op jit(solution)/shard_map/all_to_all | solution.py:81
  44.3 33.6 %all-gather.3.cloned.1.call-start = ((), (), s32[]{:S(2)}) async-start(), calls=%async_computation.4 | async-start | bytes 2027520 | tf_op jit(solution)/shard_map/all_gather | solution.py:86
  58.8 80.1 %reduce-scatter.2.cloned.1.call-start = ((), (), s32[]{:S(2)}) async-start(), calls=%async_computation.6 | async-start | bytes 2027520 | tf_op jit(solution)/shard_map/reduce_scatter | solution.py:92
  88.2 1.0 copy-start.5
  89.2 13.1 %copy-start.3 = (bf16[264,3072]{1,0:T(8,128)(2,1)S(1)}, bf16[264,3072]{1,0:T(8,128)(2,1)}, u32[]{:S(2)}) copy-start(bf16[264,3072]{1,0:T(8,128)(2,1)} %all-gather.5.cloned.1.call-done) | copy-start | bytes 4866052
  120.9 25.4 %copy-start.4 = (bf16[264,3072]{1,0:T(8,128)(2,1)S(1)}, bf16[264,3072]{1,0:T(8,128)(2,1)}, u32[]{:S(2)}) copy-start(bf16[264,3072]{1,0:T(8,128)(2,1)} %all-gather.3.cloned.1.call-done) | copy-start | bytes 4866052
  140.8 19.7 %all-to-all-start.2 = ((bf16[8,33,768]{2,1,0:T(8,128)(2,1)}), bf16[8,33,768]{2,1,0:T(8,128)(2,1)S(1)}, u32[]{:S(2)}, u32[]{:S(2)}) async-start(bf16[8,33,768]{2,1,0:T(8,128)(2,1)} %convert_element_type.50), calls=%async_computation.3 | async-start | bytes 983040 | tf_op jit(solution)/shard_map/all_to_all | solution.py:95
Sparse Core Ops, SparseCore 0:
  36.6 18.9 all-gather.4
  58.9 18.9 all-gather.2
  102.5 28.4 reduce-scatter.1
where the time goes:
time: 171 us; the launch traced here: 170 us
  matrix products  68.4 us (40%)
  local copies, waits for them, and re-layouts  34 us (20%)
  blocking collectives  20.9 us (12%)
  waiting for transfers between devices  19.8 us (12%)
  between operations  14 us (8%)
  starting transfers between devices  9.4 us (5%)
  other arithmetic  3.91 us (2%)
    dot_general x2, matrix products, contract_first(): lax.dot_general(left, right, (((0,), (0,)), ((), ())), preferred_element_...  30.7 us
    dot_general x2, matrix products, contract_last(): lax.dot_general(left, right, (((1,), (1,)), ((), ())), preferred_element_...  23.4 us
    all_to_all x1, blocking collectives, shards(): lax.all_to_all(sent_rows, 'dp', split_axis=0, concat_axis=0, tiled=True)  20.9 us
    broadcast_in_dim x1, local copies, waits for them, and re-layouts, shards(): up_total[None]  18 us
    dot_general x1, matrix products, expert_work(): jnp.dot(expert_rows, paired_weights, preferred_element_type=jnp.float32)  14.4 us
    all_to_all x1, waiting for transfers between devices, shards(): lax.all_to_all(sent_grads, 'dp', split_axis=0, concat_axis=0, tiled=True)  13.2 us
    all_to_all x1, starting transfers between devices, shards(): lax.all_to_all(summed.reshape(dp_size, CAP, narrow).astype(jnp.bfloat16),...  5.52 us
    all_gather x1, waiting for transfers between devices, shards(): lax.all_gather(got_grads.reshape(dp_size * CAP, narrow), 'tensor', axis=1...  4.52 us
  transfers between devices with their start and end apart: 5, of which 3 were waited for; matrix products, arithmetic and copies ran while one was open for 40% of the time, Pallas kernels for 0%

commit v1 on v0

v1 whole, which is shorter than its diff:
```python
import functools

import jax
import jax.numpy as jnp
from jax import lax
from jax.experimental import pallas as pl
from jax.experimental.pallas import tpu as pltpu
from jax.sharding import PartitionSpec as P

EXPERTS = 8
TOP = 2
CAP = 33
MAIN = 32
LANES = 128
BF16 = jnp.bfloat16
F32 = jnp.float32
MIB = 1 << 20


def dot(left, right, left_dim, right_dim):
    return lax.dot_general(
        left, right, (((left_dim,), (right_dim,)), ((), ())), preferred_element_type=F32
    )


def message_rows(width):
    blocks = width // LANES
    return blocks * MAIN + -(-blocks // 8) * 8


def lanes(start):
    return pl.ds(pl.multiple_of(start, LANES), LANES)


def select_rows(ids):
    count = ids.shape[1]
    expert = lax.broadcasted_iota(jnp.int32, (EXPERTS, count), 0)
    hit = ids[0:1] == expert
    for choice in range(1, TOP):
        hit = hit | (ids[choice : choice + 1] == expert)
    earlier = lax.broadcasted_iota(jnp.int32, (count, count), 0) < lax.broadcasted_iota(
        jnp.int32, (count, count), 1
    )
    rank = dot(hit.astype(F32).astype(BF16), earlier.astype(F32).astype(BF16), 1, 0)
    rank = jnp.where(hit, rank, -1.0)
    place = lax.broadcasted_iota(jnp.int32, (MAIN, count), 0).astype(F32)
    rows = [(rank[e : e + 1] == place).astype(F32) for e in range(EXPERTS)]
    rows.append((rank == float(MAIN)).astype(F32))
    return jnp.concatenate(rows, axis=0)


def row_weights(ids, probs, picks):
    count = ids.shape[1]
    expert = lax.broadcasted_iota(jnp.int32, (EXPERTS, count), 0)
    weight = jnp.zeros((EXPERTS, count), F32)
    for choice in range(TOP):
        weight = weight + jnp.where(
            ids[choice : choice + 1] == expert, probs[choice : choice + 1], 0.0
        )
    spread = [jnp.broadcast_to(weight[e : e + 1], (MAIN, count)) for e in range(EXPERTS)]
    spread = jnp.concatenate(spread + [weight], axis=0)
    return jnp.sum(spread * picks, axis=1, keepdims=True)


def pack(out_ref, rows):
    count, width = out_ref.shape[0], rows.shape[1]
    blocks = width // LANES
    left = out_ref.shape[1] - blocks * MAIN
    for i in range(count):
        for c in range(blocks):
            piece = rows[i * MAIN : (i + 1) * MAIN, c * LANES : (c + 1) * LANES]
            out_ref[i, c * MAIN : (c + 1) * MAIN, :] = piece.astype(BF16)
        last = rows[count * MAIN + i : count * MAIN + i + 1]
        lines = [last[:, c * LANES : (c + 1) * LANES] for c in range(blocks)]
        lines.append(jnp.zeros((left - blocks, LANES), F32))
        out_ref[i, blocks * MAIN :, :] = jnp.concatenate(lines, axis=0).astype(BF16)


def unpack(out_ref, message_ref, width, start):
    count = message_ref.shape[0]
    blocks = width // LANES
    last = [message_ref[i, blocks * MAIN :, :].astype(F32) for i in range(count)]
    for c in range(blocks):
        place = lanes(start + c * LANES)
        for i in range(count):
            out_ref[i * MAIN : (i + 1) * MAIN, place] = message_ref[i, c * MAIN : (c + 1) * MAIN, :]
        lines = jnp.concatenate([piece[c : c + 1] for piece in last], axis=0)
        out_ref[count * MAIN :, place] = lines.astype(BF16)


def vmem_spec():
    return pl.BlockSpec(memory_space=pltpu.VMEM)


def smem_spec():
    return pl.BlockSpec(memory_space=pltpu.SMEM)


def params(mib):
    return pltpu.CompilerParams(vmem_limit_bytes=mib * MIB)


def cost(flops, nbytes):
    return pl.CostEstimate(flops=int(flops), bytes_accessed=int(nbytes), transcendentals=0)


def whole(shape):
    return pl.BlockSpec(shape, lambda i: (0,) * len(shape), pipeline_mode=pl.Buffered(1))


def in_hbm(array):
    return pltpu.with_memory_space_constraint(array, pltpu.HBM)


def pack_messages(ids, probs, tokens, grads):
    def body(ids_ref, probs_ref, tokens_ref, grads_ref, token_out, grad_out):
        ids_in = ids_ref[...]
        picks = select_rows(ids_in)
        scale = row_weights(ids_in, probs_ref[...], picks)
        picks = picks.astype(BF16)
        pack(token_out, dot(picks, tokens_ref[...], 1, 0))
        pack(grad_out, dot(picks, grads_ref[...], 1, 0) * scale)

    shape = (EXPERTS, message_rows(grads.shape[1]), LANES)
    arrays = (ids, probs, tokens, grads)
    return pl.pallas_call(
        body,
        grid=(1,),
        in_specs=[whole(array.shape) for array in arrays],
        out_specs=[whole(shape)] * 2,
        out_shape=[jax.ShapeDtypeStruct(shape, BF16)] * 2,
        compiler_params=params(8),
        name="pack_messages",
    )(*[in_hbm(array) for array in arrays])


def combine(ids, messages, slices, width):
    count = ids.shape[1]

    def body(ids_ref, message_ref, out_ref, rows_ref):
        picks = select_rows(ids_ref[...]).astype(BF16)
        total = jnp.zeros((count, width), F32)
        for s in range(slices):
            unpack(rows_ref, message_ref.at[s], width, 0)
            total = total + dot(picks, rows_ref[...], 0, 0)
        out_ref[...] = total.astype(BF16)

    return pl.pallas_call(
        body,
        in_specs=[vmem_spec()] * 2,
        out_specs=vmem_spec(),
        out_shape=jax.ShapeDtypeStruct((count, width), BF16),
        scratch_shapes=[pltpu.VMEM((EXPERTS * CAP, width), BF16)],
        compiler_params=params(16),
        name="combine",
    )(ids, messages)


IN_FLIGHT = 13 * MIB


class Stream:
    def __init__(self, *groups):
        self.copies, self.blocks, self.sizes, self.before = [], [], [], []
        for sources, held, sems in groups:
            slots, first = held.shape[0], len(self.copies)
            for i, source in enumerate(sources):
                slot = i % slots
                self.copies.append(pltpu.make_async_copy(source, held.at[slot], sems.at[slot]))
                self.blocks.append(held.at[slot])
                self.sizes.append(2 * held.shape[1] * held.shape[2])
                self.before.append(first + i - slots if i >= slots else -1)
        self.started = self.arrived = self.used = 0
        self.start()

    def start(self):
        while self.started < len(self.copies):
            flying = sum(self.sizes[self.arrived : self.started + 1])
            if self.before[self.started] >= self.used or flying > IN_FLIGHT:
                break
            self.copies[self.started].start()
            self.started += 1

    def next(self, count):
        self.used = self.arrived
        self.start()
        first = self.arrived
        for i in range(first, first + count):
            if i >= self.started:
                self.copies[i].start()
                self.started += 1
            self.copies[i].wait()
        self.arrived += count
        self.start()
        return self.blocks[first : first + count]


def buffers(slots, *block):
    return [pltpu.VMEM((slots, *block), BF16), pltpu.SemaphoreType.DMA((slots,))]


def feature_block(ref, index, k, width, cols):
    start = pl.multiple_of((index ^ k) * width, LANES)
    return ref.at[0, pl.ds(start, width), cols]


def feature_cols(ref, index, k, width, rows):
    start = pl.multiple_of((index ^ k) * width, LANES)
    return ref.at[0, rows, pl.ds(start, width)]


def chunk_of(total):
    return min(512, total)


def chunks(total):
    step = chunk_of(total)
    return [pl.ds(j, step) for j in range(0, total, step)]


def any_specs(count):
    return [pl.BlockSpec(memory_space=pl.ANY)] * count


def gate_up_first(index, parts, w_gate, w_up, rows, width):
    hidden_units = w_gate.shape[2]
    n = len(parts)

    def body(index_ref, *refs):
        part_refs = refs[:n]
        w_gate_ref, w_up_ref, gate_ref, up_ref, x_ref, held_ref, sems = refs[n:]
        at = index_ref[0]
        sources = [
            feature_block(ref, at, k, width, cols)
            for cols in chunks(hidden_units)
            for ref in (w_gate_ref, w_up_ref)
            for k in range(n)
        ]
        stream = Stream((sources, held_ref, sems))
        for k in range(n):
            unpack(x_ref, part_refs[k], width, k * width)
        for cols in chunks(hidden_units):
            blocks = stream.next(2 * n)
            for i, out_ref in enumerate((gate_ref, up_ref)):
                value = None
                for k in range(n):
                    more = dot(x_ref[:, k * width : (k + 1) * width], blocks[i * n + k][...], 1, 0)
                    value = more if value is None else value + more
                out_ref[:, cols] = value

    wide = jax.ShapeDtypeStruct((rows, hidden_units), F32)
    return pl.pallas_call(
        body,
        grid=(1,),
        in_specs=[smem_spec()] + [whole(part.shape) for part in parts] + any_specs(2),
        out_specs=[vmem_spec()] * 2,
        out_shape=[wide, wide],
        scratch_shapes=[
            pltpu.VMEM((rows, n * width), BF16),
            *buffers(6 * n, width, chunk_of(hidden_units)),
        ],
        compiler_params=params(20),
        cost_estimate=cost(
            4 * n * rows * width * hidden_units, 4 * n * width * hidden_units
        ),
        name="gate_up_first",
    )(index, *parts, in_hbm(w_gate), in_hbm(w_up))


def hidden_state(index, parts, gate_up, w_gate, w_up, rows, width):
    hidden_units = w_gate.shape[2]
    n = len(parts)
    early = 2
    late = n - early

    def body(index_ref, *refs):
        part_refs = refs[:n]
        gate_in, up_in, w_gate_ref, w_up_ref, x_out, hidden_out = refs[n : n + 6]
        slope_ref, silu_ref, x_ref, hidden_ref, held_ref, sems, out_sems = refs[n + 6 :]
        at = index_ref[0]
        sources = [
            feature_block(ref, at, k, width, cols)
            for cols in chunks(hidden_units)
            for ref in (w_gate_ref, w_up_ref)
            for k in range(early, n)
        ]
        stream = Stream((sources, held_ref, sems))
        for k in range(n):
            unpack(x_ref, part_refs[k], width, (at ^ k) * width)
        x_copy = pltpu.make_async_copy(x_ref, x_out, out_sems.at[0])
        x_copy.start()
        for cols in chunks(hidden_units):
            values = []
            blocks = stream.next(2 * late)
            for i, before in enumerate((gate_in, up_in)):
                value = before[:, cols]
                for k in range(early, n):
                    place = pl.ds(pl.multiple_of((at ^ k) * width, LANES), width)
                    block = blocks[i * late + k - early]
                    value = value + dot(x_ref[:, place], block[...], 1, 0)
                values.append(value)
            gate, up = values
            sig = jax.nn.sigmoid(gate)
            silu = gate * sig
            hidden_ref[:, cols] = (silu * up).astype(BF16)
            slope_ref[:, cols] = (up * sig * (1.0 + gate * (1.0 - sig))).astype(BF16)
            silu_ref[:, cols] = silu.astype(BF16)
        hidden_copy = pltpu.make_async_copy(hidden_ref, hidden_out, out_sems.at[1])
        hidden_copy.start()
        x_copy.wait()
        hidden_copy.wait()

    wide = (rows, hidden_units)
    return pl.pallas_call(
        body,
        grid=(1,),
        in_specs=[smem_spec()]
        + [whole(part.shape) for part in parts]
        + [vmem_spec()] * 2
        + any_specs(2),
        out_specs=any_specs(2) + [vmem_spec()] * 2,
        out_shape=[
            pltpu.HBM((rows, n * width), BF16),
            pltpu.HBM(wide, BF16),
            jax.ShapeDtypeStruct(wide, BF16),
            jax.ShapeDtypeStruct(wide, BF16),
        ],
        scratch_shapes=[
            pltpu.VMEM((rows, n * width), BF16),
            pltpu.VMEM(wide, BF16),
            *buffers(6 * late, width, chunk_of(hidden_units)),
            pltpu.SemaphoreType.DMA((2,)),
        ],
        compiler_params=params(24),
        cost_estimate=cost(
            4 * late * rows * width * hidden_units, 4 * late * width * hidden_units
        ),
        name="hidden_state",
    )(index, *parts, *gate_up, in_hbm(w_gate), in_hbm(w_up))


def early_grads(index, parts, w_down, early, after, rows, width):
    hidden_units = w_down.shape[1]
    n = len(parts)
    late = w_down.shape[2] // width - early

    def body(index_ref, *refs):
        part_refs = refs[:n]
        w_down_ref, _, grad_ref, late_ref, y_ref, held_ref, sems, late_sems = refs[n:]
        at = index_ref[0]
        stream = Stream(
            (
                [
                    feature_cols(w_down_ref, at, k, width, cols)
                    for cols in chunks(hidden_units)
                    for k in range(early)
                ],
                held_ref,
                sems,
            )
        )
        copies = [
            pltpu.make_async_copy(
                feature_cols(w_down_ref, at, early + k, width, slice(None)),
                late_ref.at[k],
                late_sems.at[k],
            )
            for k in range(late)
        ]
        for k in range(n):
            unpack(y_ref, part_refs[k], width, k * width)
        for i, cols in enumerate(chunks(hidden_units)):
            blocks = stream.next(early)
            if i == 0:
                for copy in copies:
                    copy.start()
            value = None
            for k in range(early):
                more = dot(y_ref[:, k * width : (k + 1) * width], blocks[k][...], 1, 1)
                value = more if value is None else value + more
            grad_ref[:, cols] = value
        for copy in copies:
            copy.wait()

    return pl.pallas_call(
        body,
        grid=(1,),
        in_specs=[smem_spec()] + [whole(part.shape) for part in parts] + any_specs(2),
        out_specs=[vmem_spec()] * 2,
        out_shape=[
            jax.ShapeDtypeStruct((rows, hidden_units), F32),
            pltpu.VMEM((late, hidden_units, width), BF16),
        ],
        scratch_shapes=[
            pltpu.VMEM((rows, early * width), BF16),
            *buffers(4 * early, chunk_of(hidden_units), width),
            pltpu.SemaphoreType.DMA((late,)),
        ],
        compiler_params=params(16),
        cost_estimate=cost(
            2 * early * rows * width * hidden_units, 4 * early * width * hidden_units
        ),
        name="early_grads",
    )(index, *parts, in_hbm(w_down), after)


def input_parts(index, grads, early, grad_early, w_late, slope, silu, w_gate, w_up, rows, width):
    hidden_units = w_gate.shape[2]
    n = len(grads)
    count, lines = grads[0].shape[:2]
    order = list(range(n - 1, 0, -2)) + list(range(n - 2, -1, -2))
    step = 256 if width % 256 == 0 else LANES

    def body(index_ref, *refs):
        part_refs = refs[:n]
        grad_in, late_ref, slope_ref, silu_ref, w_gate_ref, w_up_ref = refs[n : n + 6]
        y_out, gate_ref, up_ref, odd_ref, even_ref = refs[n + 6 : n + 11]
        y_ref, rows_ref, held_ref, sems, out_sem = refs[n + 11 :]
        at = index_ref[0]
        sources = [
            feature_block(ref, at, k, width, slice(None))
            for k in order
            for ref in (w_gate_ref, w_up_ref)
        ]
        stream = Stream((sources, held_ref, sems))
        for k in range(n):
            unpack(y_ref, part_refs[k], width, (at ^ k) * width)
        y_copy = pltpu.make_async_copy(y_ref, y_out, out_sem)
        y_copy.start()
        for cols in chunks(hidden_units):
            grad = grad_in[:, cols]
            for k in range(early, n):
                place = pl.ds(pl.multiple_of((at ^ k) * width, LANES), width)
                grad = grad + dot(y_ref[:, place], late_ref[k - early, cols, :], 1, 1)
            gate_ref[:, cols] = (grad * slope_ref[:, cols].astype(F32)).astype(BF16)
            up_ref[:, cols] = (grad * silu_ref[:, cols].astype(F32)).astype(BF16)
        for i in range(n):
            gate_block, up_block = stream.next(2)
            for j in range(0, width, step):
                value = dot(gate_ref[...], gate_block[j : j + step, :], 1, 1)
                value = value + dot(up_ref[...], up_block[j : j + step, :], 1, 1)
                rows_ref[:, j : j + step] = value
            out_ref = odd_ref if i < n // 2 else even_ref
            pack(out_ref.at[i % (n // 2)], rows_ref[...])
        y_copy.wait()

    wide = jax.ShapeDtypeStruct((rows, hidden_units), BF16)
    messages = jax.ShapeDtypeStruct((n // 2, count, lines, LANES), BF16)
    return pl.pallas_call(
        body,
        grid=(1,),
        in_specs=[smem_spec()]
        + [whole(part.shape) for part in grads]
        + [vmem_spec()] * 4
        + any_specs(2),
        out_specs=any_specs(1) + [vmem_spec()] * 4,
        out_shape=[pltpu.HBM((rows, n * width), BF16), wide, wide, messages, messages],
        scratch_shapes=[
            pltpu.VMEM((rows, n * width), BF16),
            pltpu.VMEM((rows, width), F32),
            *buffers(6, width, hidden_units),
            pltpu.SemaphoreType.DMA,
        ],
        compiler_params=params(32),
        cost_estimate=cost(
            (4 * n + 2 * (n - early)) * rows * width * hidden_units,
            4 * n * width * hidden_units,
        ),
        name="input_parts",
    )(
        index,
        *grads,
        grad_early,
        pltpu.with_memory_space_constraint(w_late, pltpu.VMEM),
        slope,
        silu,
        in_hbm(w_gate),
        in_hbm(w_up),
    )


def weight_grad(left, right, name):
    rows, out_rows = left.shape
    out_cols = right.shape[1]
    tile = min(512, out_rows)
    step = min(512, out_cols)

    def body(left_ref, right_ref, out_ref):
        for j in range(out_cols // step):
            cols = slice(j * step, (j + 1) * step)
            out_ref[0, :, cols] = dot(left_ref[...], right_ref[:, cols], 0, 0).astype(BF16)

    return pl.pallas_call(
        body,
        grid=(out_rows // tile,),
        in_specs=[
            pl.BlockSpec((rows, tile), lambda i: (0, i)),
            pl.BlockSpec((rows, out_cols), lambda i: (0, 0)),
        ],
        out_specs=pl.BlockSpec((1, tile, out_cols), lambda i: (0, i, 0)),
        out_shape=jax.ShapeDtypeStruct((1, out_rows, out_cols), BF16),
        compiler_params=params(32),
        cost_estimate=cost(4 * rows * out_rows * out_cols, 2 * out_rows * out_cols),
        name=name,
    )(left, right)


def tie(array, after):
    def body(array_ref, after_ref, out_ref):
        del array_ref, after_ref, out_ref

    return pl.pallas_call(
        body,
        in_specs=any_specs(2),
        out_specs=pl.BlockSpec(memory_space=pl.ANY),
        out_shape=jax.ShapeDtypeStruct(array.shape, array.dtype),
        input_output_aliases={0: 0},
        compiler_params=params(1),
        name="tie",
    )(array, after)


def across(array, distance, size):
    return lax.ppermute(array, "tensor", [(i, i ^ distance) for i in range(size)])


def exchange(messages):
    return lax.all_to_all(messages, "dp", split_axis=0, concat_axis=0, tiled=True)


def gather_parts(own, size, after=None):
    parts = [own] + [None] * (size - 1)
    for k in range(2, size, 2):
        parts[k] = across(own, k, size)
        if after is not None:
            parts[k] = tie(parts[k], after)
    for k in range(0, size, 2):
        parts[k + 1] = across(parts[k], 1, size)
    return parts


def shards(tokens, grad_out, expert_ids, gate_probs, w_gate, w_up, w_down):
    dp_size = lax.axis_size("dp")
    size = lax.axis_size("tensor")
    slices = dp_size // EXPERTS
    width = tokens.shape[1]
    rows = dp_size * CAP
    index = lax.axis_index("tensor").astype(jnp.int32).reshape(1)
    ids = expert_ids.T
    probs = gate_probs.T

    def spread(messages):
        return messages if slices == 1 else jnp.repeat(messages, slices, axis=0)

    early = 2
    token_messages, grad_messages = pack_messages(ids, probs, tokens, grad_out)
    token_parts = gather_parts(exchange(spread(token_messages)), size)
    own_grads = exchange(spread(grad_messages))
    first = gate_up_first(index, token_parts[:early], w_gate, w_up, rows, width)
    x, hidden, slope, silu = hidden_state(index, token_parts, first, w_gate, w_up, rows, width)
    grad_parts = gather_parts(tie(own_grads, first[0]), size, slope)
    grad_early, w_late = early_grads(
        index, grad_parts[:early], w_down, early, slope, rows, width
    )
    y, gate_grad, up_grad, odd, even = input_parts(
        index, grad_parts, early, grad_early, w_late, slope, silu, w_gate, w_up, rows, width
    )
    sums = even.astype(F32) + across(odd, 1, size).astype(F32)
    total = sums[-1]
    for i, k in enumerate(range(size - 2, 0, -2)):
        total = total + across(sums[i].astype(BF16), k, size).astype(F32)
    back = exchange(total.astype(BF16))
    grad_down = weight_grad(hidden, y, "down_grad")
    grad_gate = weight_grad(x, gate_grad, "gate_grad")
    grad_up = weight_grad(x, up_grad, "up_grad")
    by_slice = back.reshape((EXPERTS, slices) + back.shape[1:]).swapaxes(0, 1)
    input_grad = combine(ids, by_slice, slices, width)
    return (input_grad, grad_gate, grad_up, grad_down)


def solution(mesh):
    placed = (
        P("dp", "tensor"),
        P("dp", "tensor"),
        P("dp", None),
        P("dp", None),
        P("dp", None, "tensor"),
        P("dp", None, "tensor"),
        P("dp", "tensor", None),
    )
    return jax.shard_map(
        shards,
        mesh=mesh,
        in_specs=placed,
        out_specs=(
            P("dp", "tensor"),
            P("dp", None, "tensor"),
            P("dp", None, "tensor"),
            P("dp", "tensor", None),
        ),
        check_vma=False,
    )
```

time: 171 us -> 111 us (0.65)
  matrix products: 68.4 us -> 0 us
  Pallas kernels: 0 us -> 66.2 us
  local copies, waits for them, and re-layouts: 34 us -> 2.84 us
  between operations: 14 us -> 0.79 us
  waiting for transfers between devices: 19.8 us -> 8.7 us
  other arithmetic: 3.91 us -> 1.02 us
  starting transfers between devices: 9.4 us -> 11.5 us
    dot_general x5 -> x0, matrix products: 68.4 us -> none  [the longest x2 30.7 us: contract_first(): lax.dot_general(left, right, (((0,), (0,)), ((), ())), preferred_element_...]
    pallas_call x0 -> x11, Pallas kernels: none -> 66.2 us  [the longest x3 27.7 us: weight_grad(): pl.pallas_call(body, grid=(out_rows // tile,), in_specs=[pl.BlockSpec((ro...]
    broadcast_in_dim x1 -> x0, local copies, waits for them, and re-layouts: 18 us -> none  [shards(): up_total[None]]
    all_to_all x2, waiting for transfers between devices: 15.2 us -> 1.13 us  [exchange(): lax.all_to_all(messages, 'dp', split_axis=0, concat_axis=0, tiled=True)]
    ppermute x0 -> x8, waiting for transfers between devices: none -> 7.58 us  [across(): lax.ppermute(array, 'tensor', [(i, i ^ distance) for i in range(size)])]
    gather x6 -> x0, local copies, waits for them, and re-layouts: 6.87 us -> none  [the longest x2 3 us: shards(): padded(product.astype(jnp.bfloat16).reshape(pair_count, grad_out.shape[1]))]
    all_gather x2 -> x0, waiting for transfers between devices: 4.54 us -> none  [the longest x1 4.52 us: shards(): lax.all_gather(got_grads.reshape(dp_size * CAP, narrow), 'tensor', axis=1...]
    ppermute x0 -> x8, starting transfers between devices: none -> 3.6 us  [across(): lax.ppermute(array, 'tensor', [(i, i ^ distance) for i in range(size)])]
  transfers between devices with their start and end apart: 5 -> 10, of which waited for: 3 -> 4; matrix products, arithmetic and copies ran while one was open for 40% -> 0% of each run, Pallas kernels for 0% -> 44%
where the time goes in v1:
time: 111 us; the launch traced here: 110 us
  Pallas kernels  66.2 us (60%)
  blocking collectives  19.4 us (17%)
  starting transfers between devices  11.5 us (10%)
  waiting for transfers between devices  8.7 us (8%)
  local copies, waits for them, and re-layouts  2.84 us (3%)
    pallas_call x3, Pallas kernels, weight_grad(): pl.pallas_call(body, grid=(out_rows // tile,), in_specs=[pl.BlockSpec((ro...  27.7 us
    all_to_all x1, blocking collectives, exchange(): lax.all_to_all(messages, 'dp', split_axis=0, concat_axis=0, tiled=True)  19.4 us
    pallas_call x1, Pallas kernels, input_parts(): pl.pallas_call(body, grid=(1,), in_specs=[smem_spec()] + [whole(part.shap...  14.2 us
    pallas_call x1, Pallas kernels, hidden_state(): pl.pallas_call(body, grid=(1,), in_specs=[smem_spec()] + [whole(part.shap...  9.73 us
    all_to_all x2, starting transfers between devices, exchange(): lax.all_to_all(messages, 'dp', split_axis=0, concat_axis=0, tiled=True)  7.85 us
    ppermute x8, waiting for transfers between devices, across(): lax.ppermute(array, 'tensor', [(i, i ^ distance) for i in range(size)])  7.58 us
    pallas_call x1, Pallas kernels, gate_up_first(): pl.pallas_call(body, grid=(1,), in_specs=[smem_spec()] + [whole(part.shap...  6.1 us
    pallas_call x1, Pallas kernels, early_grads(): pl.pallas_call(body, grid=(1,), in_specs=[smem_spec()] + [whole(part.shap...  5.05 us
  transfers between devices with their start and end apart: 10, of which 4 were waited for; matrix products, arithmetic and copies ran while one was open for 0% of the time, Pallas kernels for 44%

profile of v1, /device:TPU:0, one launch (start us, length us, event | category | flops | bytes accessed | tf_op | source)
XLA Modules:
  0.0 110.4 jit_solution(1791366218589060314)
XLA Ops:
  0.6 2.3 %pack_messages.1 = (bf16[8,200,128]{2,1,0:T(8,128)(2,1)S(1)}, bf16[8,200,128]{2,1,0:T(8,128)(2,1)}) custom-call(s32[2,128]{1,0:T(2,128)} %bitcast.13, f32[2,128]{1,0:T(2,128)} %bitcast.15, bf16[128,768]{1,0:T(8,128)(2,1)} %tokens_ref.1, bf16[128,768]{1,0:T(8,128)(2,1)} %grads_ref.1), custom_call_target="tpu_custom_call" | custom-call | tf_op jit(solution)/shard_map/pack_messages/pallas_call | solution.py:126
  2.9 19.4 %all_to_all.15.refs_0_ = bf16[8,200,128]{2,1,0:T(8,128)(2,1)S(1)} all-to-all(bf16[8,200,128]{2,1,0:T(8,128)(2,1)S(1)} %get-tuple-element.20), channel_id=1, replica_groups=mesh['dp'=8,'tensor'=4] {'dp'}, dimensions={0} | all-to-all | bytes 819200 | tf_op jit(solution)/shard_map/all_to_all | solution.py:528
  22.4 1.5 %collective-permute-start.3 = (bf16[8,200,128]{2,1,0:T(8,128)(2,1)S(1)}, bf16[8,200,128]{2,1,0:T(8,128)(2,1)}, u32[]{:S(2)}, u32[]{:S(2)}) collective-permute-start(bf16[8,200,128]{2,1,0:T(8,128)(2,1)S(1)} %all_to_all.15.refs_0_), channel_id=1, source_target_pairs={{0,2},{1,3},{2,0},{3,1},{4,6},{5,7},{6,4},{7,5},{8,10},{9,11},{10,... | collective-permute-start | bytes 1228808 | tf_op jit(solution)/shard_map/ppermute | solution.py:524
  23.9 0.0 collective-permute-start
  23.9 3.5 %all-to-all-start = ((bf16[8,200,128]{2,1,0:T(8,128)(2,1)}), bf16[8,200,128]{2,1,0:T(8,128)(2,1)S(1)}, u32[]{:S(2)}, u32[]{:S(2)}) async-start(bf16[8,200,128]{2,1,0:T(8,128)(2,1)} %get-tuple-element.19), calls=%async_computation | async-start | bytes 819200 | tf_op jit(solution)/shard_map/all_to_all | solution.py:528
  27.3 4.3 %collective-permute-done.3.refs_2_ = bf16[8,200,128]{2,1,0:T(8,128)(2,1)} collective-permute-done((bf16[8,200,128]{2,1,0:T(8,128)(2,1)S(1)}, bf16[8,200,128]{2,1,0:T(8,128)(2,1)}, u32[]{:S(2)}, u32[]{:S(2)}) %collective-permute-start.3) | collective-permute-done | bytes 409632 | tf_op jit(solution)/shard_map/ppermute | solution.py:524
  31.7 0.0 collective-permute-start.4
  31.7 0.0 collective-permute-done.refs_1_
  31.7 6.1 %gate_up_first.1 = (f32[264,2048]{1,0:T(8,128)S(1)}, f32[264,2048]{1,0:T(8,128)S(1)}) custom-call(s32[1]{0:T(128)} %bitcast.1.index_ref, bf16[8,200,128]{2,1,0:T(8,128)(2,1)S(1)} %all_to_all.15.refs_0_, bf16[8,200,128]{2,1,0:T(8,128)(2,1)S(1)} %collective-permute-done.refs_1_, bf16[1,3072,2048]{2,1,0:T(8,128)(2,1)} %refs_8_.1, bf16[1,3072,2048]{2,1,0:T(8,128)(2,1)} %refs_9_.1), custom_call_target="tpu_custom_call" | custom-call | flops 3321888768 | bytes 12582912 | tf_op jit(solution)/shard_map/gate_up_first/pallas_call | solution.py:252
  37.8 0.0 copy-start
  37.8 1.3 %copy-done = f32[264,2048]{1,0:T(8,128)} copy-done((f32[264,2048]{1,0:T(8,128)}, f32[264,2048]{1,0:T(8,128)S(1)}, u32[]{:S(2)}) %copy-start) | copy-done | bytes 2162712
  39.1 1.1 %all-to-all-done.array_ref = bf16[8,200,128]{2,1,0:T(8,128)(2,1)S(1)} async-done(((bf16[8,200,128]{2,1,0:T(8,128)(2,1)}), bf16[8,200,128]{2,1,0:T(8,128)(2,1)S(1)}, u32[]{:S(2)}, u32[]{:S(2)}) %all-to-all-start) | async-done | bytes 409632 | tf_op jit(solution)/shard_map/all_to_all | solution.py:528
  40.2 0.0 copy-start.1
  40.2 0.5 collective-permute-start.2
  40.8 0.1 collective-permute-start.1
  40.9 0.0 collective-permute-done.4.refs_3_
  40.9 1.0 copy-done.1
  41.9 9.7 %hidden_state.1 = (bf16[264,3072]{1,0:T(8,128)(2,1)}, bf16[264,2048]{1,0:T(8,128)(2,1)}, bf16[264,2048]{1,0:T(8,128)(2,1)S(1)}, bf16[264,2048]{1,0:T(8,128)(2,1)S(1)}) custom-call(s32[1]{0:T(128)} %bitcast.1.index_ref, bf16[8,200,128]{2,1,0:T(8,128)(2,1)S(1)} %all_to_all.15.refs_0_, bf16[8,200,128]{2,1,0:T(8,128)(2,1)S(1)} %collective-permute-done.refs_1_, ...), custom_call_target="tpu_custom_call" | custom-call | flops 3321888768 | bytes 12582912 | tf_op jit(solution)/shard_map/hidden_state/pallas_call | solution.py:314
  51.6 0.0 collective-permute-done.2.array_ref
  51.6 0.1 collective-permute-start.5
  51.7 0.0 collective-permute-done.1.refs_1_
  51.7 5.0 %early_grads.1 = (f32[264,2048]{1,0:T(8,128)S(1)}, bf16[2,2048,768]{2,1,0:T(8,128)(2,1)S(1)}) custom-call(s32[1]{0:T(128)} %bitcast.1.index_ref, bf16[8,200,128]{2,1,0:T(8,128)(2,1)S(1)} %tie.2.refs_0_, bf16[8,200,128]{2,1,0:T(8,128)(2,1)S(1)} %collective-permute-done.1.refs_1_, bf16[1,2048,3072]{2,1,0:T(8,128)(2,1)} %refs_2_.3, ...), custom_call_target="tpu_custom_call" | custom-call | flops 1660944384 | bytes 12582912 | tf_op jit(solution)/shard_map/early_grads/pallas_call | solution.py:385
  56.8 0.0 collective-permute-done.5.refs_3_
  56.8 14.2 %input_parts.1 = (bf16[264,3072]{1,0:T(8,128)(2,1)}, bf16[264,2048]{1,0:T(8,128)(2,1)S(1)}, bf16[264,2048]{1,0:T(8,128)(2,1)S(1)}, bf16[2,8,200,128]{3,2,1,0:T(8,128)(2,1)S(1)}, bf16[2,8,200,128]{3,2,1,0:T(8,128)(2,1)S(1)}) custom-call(s32[1]{0:T(128)} %bitcast.1.index_ref, bf16[8,200,128]{2,1,0:T(8,128)(2,1)S(1)} %tie.2.refs_0_, ...), custom_call_target="tpu_custom_call" | custom-call | flops 8304721920 | bytes 25165824 | tf_op jit(solution)/shard_map/input_parts/pallas_call | solution.py:449
  71.0 0.0 copy-start.6
  71.0 0.7 collective-permute-start.6
  71.7 2.0 %collective-permute-done.6 = bf16[2,8,200,128]{3,2,1,0:T(8,128)(2,1)S(1)} collective-permute-done((bf16[2,8,200,128]{3,2,1,0:T(8,128)(2,1)S(1)}, bf16[2,8,200,128]{3,2,1,0:T(8,128)(2,1)S(1)}, u32[]{:S(2)}, u32[]{:S(2)}) %collective-permute-start.6) | collective-permute-done | bytes 819232 | tf_op jit(solution)/shard_map/ppermute | solution.py:524
  73.6 0.0 copy-start.3
  73.6 0.2 convert_add_fusion
  73.8 0.0 copy-done.6
  73.8 0.1 fusion.2
  73.9 0.8 collective-permute-start.7
  74.6 0.4 copy-done.3
  75.0 9.3 %gate_grad.1 = bf16[1,3072,2048]{2,1,0:T(8,128)(2,1)} custom-call(bf16[264,3072]{1,0:T(8,128)(2,1)S(1)} %copy-done.3, bf16[264,2048]{1,0:T(8,128)(2,1)S(1)} %get-tuple-element.30.right_ref), custom_call_target="tpu_custom_call" | custom-call | flops 6643777536 | bytes 12582912 | tf_op jit(solution)/shard_map/gate_grad/pallas_call | solution.py:493
  84.4 0.0 copy-start.7
  84.4 1.3 %collective-permute-done.7 = bf16[8,200,128]{2,1,0:T(8,128)(2,1)S(1)} collective-permute-done((bf16[8,200,128]{2,1,0:T(8,128)(2,1)S(1)}, bf16[8,200,128]{2,1,0:T(8,128)(2,1)S(1)}, u32[]{:S(2)}, u32[]{:S(2)}) %collective-permute-start.7) | collective-permute-done | bytes 409632 | tf_op jit(solution)/shard_map/ppermute | solution.py:524
  85.7 0.9 fusion.1
  86.5 4.4 %all-to-all-start.2 = ((bf16[8,200,128]{2,1,0:T(8,128)(2,1)}), bf16[8,200,128]{2,1,0:T(8,128)(2,1)S(1)}, u32[]{:S(2)}, u32[]{:S(2)}) async-start(bf16[8,200,128]{2,1,0:T(8,128)(2,1)} %fusion.1), calls=%async_computation.2 | async-start | bytes 819200 | tf_op jit(solution)/shard_map/all_to_all | solution.py:528
  90.9 0.0 copy-done.7
  90.9 0.0 copy-start.4
  90.9 0.0 copy-start.5
  90.9 9.2 %up_grad.1 = bf16[1,3072,2048]{2,1,0:T(8,128)(2,1)} custom-call(bf16[264,3072]{1,0:T(8,128)(2,1)S(1)} %copy-done.3, bf16[264,2048]{1,0:T(8,128)(2,1)S(1)} %copy-done.7), custom_call_target="tpu_custom_call" | custom-call | flops 6643777536 | bytes 12582912 | tf_op jit(solution)/shard_map/up_grad/pallas_call | solution.py:493
  100.2 0.0 copy-done.4
  100.2 0.0 copy-done.5
  100.2 0.0 copy-start.2
  100.2 9.1 %down_grad.1 = bf16[1,2048,3072]{2,1,0:T(8,128)(2,1)} custom-call(bf16[264,2048]{1,0:T(8,128)(2,1)S(1)} %copy-done.5, bf16[264,3072]{1,0:T(8,128)(2,1)S(1)} %copy-done.4), custom_call_target="tpu_custom_call" | custom-call | flops 6643777536 | bytes 12582912 | tf_op jit(solution)/shard_map/down_grad/pallas_call | solution.py:493
  109.3 0.0 all-to-all-done.2
  109.3 0.0 copy-done.2
  109.3 1.1 %combine.1 = bf16[128,768]{1,0:T(8,128)(2,1)} custom-call(s32[2,128]{1,0:T(2,128)S(1)} %bitcast.14, bf16[1,8,200,128]{3,2,1,0:T(8,128)(2,1)S(1)} %bitcast.12), custom_call_target="tpu_custom_call" | custom-call | tf_op jit(solution)/shard_map/combine/pallas_call | solution.py:148
  (2 shorter events, 0.0 us)
Async XLA Ops:
  22.4 9.3 %collective-permute-start.3 = (bf16[8,200,128]{2,1,0:T(8,128)(2,1)S(1)}, bf16[8,200,128]{2,1,0:T(8,128)(2,1)}, u32[]{:S(2)}, u32[]{:S(2)}) collective-permute-start(bf16[8,200,128]{2,1,0:T(8,128)(2,1)S(1)} %all_to_all.15.refs_0_), channel_id=1, source_target_pairs={{0,2},{1,3},{2,0},{3,1},{4,6},{5,7},{6,4},{7,5},{8,10},{9,11},{10,... | collective-permute-start | bytes 1228808 | tf_op jit(solution)/shard_map/ppermute | solution.py:524
  23.9 7.8 %collective-permute-start = (bf16[8,200,128]{2,1,0:T(8,128)(2,1)S(1)}, bf16[8,200,128]{2,1,0:T(8,128)(2,1)S(1)}, u32[]{:S(2)}, u32[]{:S(2)}) collective-permute-start(bf16[8,200,128]{2,1,0:T(8,128)(2,1)S(1)} %all_to_all.15.refs_0_), channel_id=1, source_target_pairs={{0,1},{1,0},{2,3},{3,2},{4,5},{5,4},{6,7},{7,6},{8,9},{9,8},{10,11... | collective-permute-start | bytes 1228808 | tf_op jit(solution)/shard_map/ppermute | solution.py:524
  23.9 16.4 %all-to-all-start = ((bf16[8,200,128]{2,1,0:T(8,128)(2,1)}), bf16[8,200,128]{2,1,0:T(8,128)(2,1)S(1)}, u32[]{:S(2)}, u32[]{:S(2)}) async-start(bf16[8,200,128]{2,1,0:T(8,128)(2,1)} %get-tuple-element.19), calls=%async_computation | async-start | bytes 819200 | tf_op jit(solution)/shard_map/all_to_all | solution.py:528
  31.7 9.2 %collective-permute-start.4 = (bf16[8,200,128]{2,1,0:T(8,128)(2,1)}, bf16[8,200,128]{2,1,0:T(8,128)(2,1)}, u32[]{:S(2)}, u32[]{:S(2)}) collective-permute-start(bf16[8,200,128]{2,1,0:T(8,128)(2,1)} %collective-permute-done.3.refs_2_), channel_id=1, source_target_pairs={{0,1},{1,0},{2,3},{3,2},{4,5},{5,4},{6,7},{7,6},{8,9},{9,8},{10,11... | collective-permute-start | bytes 1228808 | tf_op jit(solution)/shard_map/ppermute | solution.py:524
  37.8 1.3 %copy-start = (f32[264,2048]{1,0:T(8,128)}, f32[264,2048]{1,0:T(8,128)S(1)}, u32[]{:S(2)}) copy-start(f32[264,2048]{1,0:T(8,128)S(1)} %get-tuple-element.22.refs_5_) | copy-start | bytes 6488068
  40.2 1.6 %copy-start.1 = (f32[264,2048]{1,0:T(8,128)S(1)}, f32[264,2048]{1,0:T(8,128)}, u32[]{:S(2)}) copy-start(f32[264,2048]{1,0:T(8,128)} %copy-done) | copy-start | bytes 6488068
  40.2 11.4 %collective-permute-start.2 = (bf16[8,200,128]{2,1,0:T(8,128)(2,1)S(1)}, bf16[8,200,128]{2,1,0:T(8,128)(2,1)S(1)}, u32[]{:S(2)}, u32[]{:S(2)}) collective-permute-start(bf16[8,200,128]{2,1,0:T(8,128)(2,1)S(1)} %tie.2.refs_0_), channel_id=1, source_target_pairs={{0,2},{1,3},{2,0},{3,1},{4,6},{5,7},{6,4},{7,5},{8,10},{9,11},{10,... | collective-permute-start | bytes 1228808 | tf_op jit(solution)/shard_map/ppermute | solution.py:524
  40.8 10.9 %collective-permute-start.1 = (bf16[8,200,128]{2,1,0:T(8,128)(2,1)S(1)}, bf16[8,200,128]{2,1,0:T(8,128)(2,1)S(1)}, u32[]{:S(2)}, u32[]{:S(2)}) collective-permute-start(bf16[8,200,128]{2,1,0:T(8,128)(2,1)S(1)} %tie.2.refs_0_), channel_id=1, source_target_pairs={{0,1},{1,0},{2,3},{3,2},{4,5},{5,4},{6,7},{7,6},{8,9},{9,8},{10,11... | collective-permute-start | bytes 1228808 | tf_op jit(solution)/shard_map/ppermute | solution.py:524
  51.6 5.1 %collective-permute-start.5 = (bf16[8,200,128]{2,1,0:T(8,128)(2,1)S(1)}, bf16[8,200,128]{2,1,0:T(8,128)(2,1)S(1)}, u32[]{:S(2)}, u32[]{:S(2)}) collective-permute-start(bf16[8,200,128]{2,1,0:T(8,128)(2,1)S(1)} %tie.3.refs_2_), channel_id=1, source_target_pairs={{0,1},{1,0},{2,3},{3,2},{4,5},{5,4},{6,7},{7,6},{8,9},{9,8},{10,11... | collective-permute-start | bytes 1228808 | tf_op jit(solution)/shard_map/ppermute | solution.py:524
  71.0 2.8 %copy-start.6 = (bf16[264,2048]{1,0:T(8,128)(2,1)}, bf16[264,2048]{1,0:T(8,128)(2,1)S(1)}, u32[]{:S(2)}) copy-start(bf16[264,2048]{1,0:T(8,128)(2,1)S(1)} %get-tuple-element.31.right_ref) | copy-start | bytes 3244036
  71.0 2.6 %collective-permute-start.6 = (bf16[2,8,200,128]{3,2,1,0:T(8,128)(2,1)S(1)}, bf16[2,8,200,128]{3,2,1,0:T(8,128)(2,1)S(1)}, u32[]{:S(2)}, u32[]{:S(2)}) collective-permute-start(bf16[2,8,200,128]{3,2,1,0:T(8,128)(2,1)S(1)} %get-tuple-element.28), channel_id=1, source_target_pairs={{0,1},{1,0},{2,3},{3,2},{4,5},{5,4},{6,7},{7,6},{8,9},{9,8},{10,11... | collective-permute-start | bytes 2457608 | tf_op jit(solution)/shard_map/ppermute | solution.py:524
  73.6 1.4 %copy-start.3 = (bf16[264,3072]{1,0:T(8,128)(2,1)S(1)}, bf16[264,3072]{1,0:T(8,128)(2,1)}, u32[]{:S(2)}) copy-start(bf16[264,3072]{1,0:T(8,128)(2,1)} %get-tuple-element.29.left_ref) | copy-start | bytes 4866052
  73.9 11.8 %collective-permute-start.7 = (bf16[8,200,128]{2,1,0:T(8,128)(2,1)S(1)}, bf16[8,200,128]{2,1,0:T(8,128)(2,1)S(1)}, u32[]{:S(2)}, u32[]{:S(2)}) collective-permute-start(bf16[8,200,128]{2,1,0:T(8,128)(2,1)S(1)} %fusion.2), channel_id=1, source_target_pairs={{0,2},{1,3},{2,0},{3,1},{4,6},{5,7},{6,4},{7,5},{8,10},{9,11},{10,... | collective-permute-start | bytes 1228808 | tf_op jit(solution)/shard_map/ppermute | solution.py:524
  84.4 6.5 %copy-start.7 = (bf16[264,2048]{1,0:T(8,128)(2,1)S(1)}, bf16[264,2048]{1,0:T(8,128)(2,1)}, u32[]{:S(2)}) copy-start(bf16[264,2048]{1,0:T(8,128)(2,1)} %copy-done.6) | copy-start | bytes 3244036
  86.5 22.8 %all-to-all-start.2 = ((bf16[8,200,128]{2,1,0:T(8,128)(2,1)}), bf16[8,200,128]{2,1,0:T(8,128)(2,1)S(1)}, u32[]{:S(2)}, u32[]{:S(2)}) async-start(bf16[8,200,128]{2,1,0:T(8,128)(2,1)} %fusion.1), calls=%async_computation.2 | async-start | bytes 819200 | tf_op jit(solution)/shard_map/all_to_all | solution.py:528
  90.9 9.3 %copy-start.4 = (bf16[264,3072]{1,0:T(8,128)(2,1)S(1)}, bf16[264,3072]{1,0:T(8,128)(2,1)}, u32[]{:S(2)}) copy-start(bf16[264,3072]{1,0:T(8,128)(2,1)} %get-tuple-element.33.right_ref) | copy-start | bytes 4866052
  90.9 9.2 %copy-start.5 = (bf16[264,2048]{1,0:T(8,128)(2,1)S(1)}, bf16[264,2048]{1,0:T(8,128)(2,1)}, u32[]{:S(2)}) copy-start(bf16[264,2048]{1,0:T(8,128)(2,1)} %get-tuple-element.32.left_ref) | copy-start | bytes 3244036
  100.2 9.1 %copy-start.2 = (s32[128,2]{0,1:T(2,128)S(1)}, s32[128,2]{0,1:T(2,128)}, u32[]{:S(2)}) copy-start(s32[128,2]{0,1:T(2,128)} %param.9) | copy-start | bytes 3076

commit v2 on v1

--- a/solution.py
+++ b/solution.py
@@ -166,7 +166,14 @@
             slots, first = held.shape[0], len(self.copies)
             for i, source in enumerate(sources):
                 slot = i % slots
-                self.copies.append(pltpu.make_async_copy(source, held.at[slot], sems.at[slot]))
+                self.copies.append(
+                    [
+                        pltpu.make_async_copy(
+                            source.at[:, cols], held.at[slot, :, cols], sems.at[slot, j]
+                        )
+                        for j, cols in enumerate(pieces(held.shape[2]))
+                    ]
+                )
                 self.blocks.append(held.at[slot])
                 self.sizes.append(2 * held.shape[1] * held.shape[2])
                 self.before.append(first + i - slots if i >= slots else -1)
@@ -178,8 +185,12 @@
             flying = sum(self.sizes[self.arrived : self.started + 1])
             if self.before[self.started] >= self.used or flying > IN_FLIGHT:
                 break
-            self.copies[self.started].start()
-            self.started += 1
+            self.start_next()
+
+    def start_next(self):
+        for copy in self.copies[self.started]:
+            copy.start()
+        self.started += 1
 
     def next(self, count):
         self.used = self.arrived
@@ -187,16 +198,27 @@
         first = self.arrived
         for i in range(first, first + count):
             if i >= self.started:
-                self.copies[i].start()
-                self.started += 1
-            self.copies[i].wait()
+                self.start_next()
+            for copy in self.copies[i]:
+                copy.wait()
         self.arrived += count
         self.start()
         return self.blocks[first : first + count]
 
 
+PIECE = 4096
+
+
+def pieces(columns):
+    step = min(PIECE, columns)
+    return [pl.ds(j, step) for j in range(0, columns, step)] if columns % step == 0 else [pl.ds(0, columns)]
+
+
 def buffers(slots, *block):
-    return [pltpu.VMEM((slots, *block), BF16), pltpu.SemaphoreType.DMA((slots,))]
+    return [
+        pltpu.VMEM((slots, *block), BF16),
+        pltpu.SemaphoreType.DMA((slots, len(pieces(block[1])))),
+    ]
 
 
 def feature_block(ref, index, k, width, cols):
@@ -251,8 +273,7 @@
     wide = jax.ShapeDtypeStruct((rows, hidden_units), F32)
     return pl.pallas_call(
         body,
-        grid=(1,),
-        in_specs=[smem_spec()] + [whole(part.shape) for part in parts] + any_specs(2),
+        in_specs=[smem_spec()] + [vmem_spec() for _ in parts] + any_specs(2),
         out_specs=[vmem_spec()] * 2,
         out_shape=[wide, wide],
         scratch_shapes=[
@@ -275,8 +296,8 @@
 
     def body(index_ref, *refs):
         part_refs = refs[:n]
-        gate_in, up_in, w_gate_ref, w_up_ref, x_out, hidden_out = refs[n : n + 6]
-        slope_ref, silu_ref, x_ref, hidden_ref, held_ref, sems, out_sems = refs[n + 6 :]
+        gate_in, up_in, w_gate_ref, w_up_ref, x_ref, hidden_ref = refs[n : n + 6]
+        slope_ref, silu_ref, held_ref, sems = refs[n + 6 :]
         at = index_ref[0]
         sources = [
             feature_block(ref, at, k, width, cols)
@@ -287,8 +308,6 @@
         stream = Stream((sources, held_ref, sems))
         for k in range(n):
             unpack(x_ref, part_refs[k], width, (at ^ k) * width)
-        x_copy = pltpu.make_async_copy(x_ref, x_out, out_sems.at[0])
-        x_copy.start()
         for cols in chunks(hidden_units):
             values = []
             blocks = stream.next(2 * late)
@@ -305,33 +324,19 @@
             hidden_ref[:, cols] = (silu * up).astype(BF16)
             slope_ref[:, cols] = (up * sig * (1.0 + gate * (1.0 - sig))).astype(BF16)
             silu_ref[:, cols] = silu.astype(BF16)
-        hidden_copy = pltpu.make_async_copy(hidden_ref, hidden_out, out_sems.at[1])
-        hidden_copy.start()
-        x_copy.wait()
-        hidden_copy.wait()
 
     wide = (rows, hidden_units)
     return pl.pallas_call(
         body,
-        grid=(1,),
         in_specs=[smem_spec()]
-        + [whole(part.shape) for part in parts]
+        + [vmem_spec() for _ in parts]
         + [vmem_spec()] * 2
         + any_specs(2),
-        out_specs=any_specs(2) + [vmem_spec()] * 2,
-        out_shape=[
-            pltpu.HBM((rows, n * width), BF16),
-            pltpu.HBM(wide, BF16),
-            jax.ShapeDtypeStruct(wide, BF16),
-            jax.ShapeDtypeStruct(wide, BF16),
-        ],
-        scratch_shapes=[
-            pltpu.VMEM((rows, n * width), BF16),
-            pltpu.VMEM(wide, BF16),
-            *buffers(6 * late, width, chunk_of(hidden_units)),
-            pltpu.SemaphoreType.DMA((2,)),
-        ],
-        compiler_params=params(24),
+        out_specs=[vmem_spec()] * 4,
+        out_shape=[jax.ShapeDtypeStruct((rows, n * width), BF16)]
+        + [jax.ShapeDtypeStruct(wide, BF16)] * 3,
+        scratch_shapes=buffers(6 * late, width, chunk_of(hidden_units)),
+        compiler_params=params(20),
         cost_estimate=cost(
             4 * late * rows * width * hidden_units, 4 * late * width * hidden_units
         ),
@@ -384,8 +389,7 @@
 
     return pl.pallas_call(
         body,
-        grid=(1,),
-        in_specs=[smem_spec()] + [whole(part.shape) for part in parts] + any_specs(2),
+        in_specs=[smem_spec()] + [vmem_spec() for _ in parts] + any_specs(2),
         out_specs=[vmem_spec()] * 2,
         out_shape=[
             jax.ShapeDtypeStruct((rows, hidden_units), F32),
@@ -414,8 +418,8 @@
     def body(index_ref, *refs):
         part_refs = refs[:n]
         grad_in, late_ref, slope_ref, silu_ref, w_gate_ref, w_up_ref = refs[n : n + 6]
-        y_out, gate_ref, up_ref, odd_ref, even_ref = refs[n + 6 : n + 11]
-        y_ref, rows_ref, held_ref, sems, out_sem = refs[n + 11 :]
+        y_ref, gate_ref, up_ref = refs[n + 6 : n + 9]
+        out_refs, (rows_ref, held_ref, sems) = refs[n + 9 : -3], refs[-3:]
         at = index_ref[0]
         sources = [
             feature_block(ref, at, k, width, slice(None))
@@ -425,8 +429,6 @@
         stream = Stream((sources, held_ref, sems))
         for k in range(n):
             unpack(y_ref, part_refs[k], width, (at ^ k) * width)
-        y_copy = pltpu.make_async_copy(y_ref, y_out, out_sem)
-        y_copy.start()
         for cols in chunks(hidden_units):
             grad = grad_in[:, cols]
             for k in range(early, n):
@@ -434,34 +436,35 @@
                 grad = grad + dot(y_ref[:, place], late_ref[k - early, cols, :], 1, 1)
             gate_ref[:, cols] = (grad * slope_ref[:, cols].astype(F32)).astype(BF16)
             up_ref[:, cols] = (grad * silu_ref[:, cols].astype(F32)).astype(BF16)
+
+        def finish(i):
+            pack(out_refs[i], rows_ref[i % 2])
+
         for i in range(n):
             gate_block, up_block = stream.next(2)
             for j in range(0, width, step):
                 value = dot(gate_ref[...], gate_block[j : j + step, :], 1, 1)
                 value = value + dot(up_ref[...], up_block[j : j + step, :], 1, 1)
-                rows_ref[:, j : j + step] = value
-            out_ref = odd_ref if i < n // 2 else even_ref
-            pack(out_ref.at[i % (n // 2)], rows_ref[...])
-        y_copy.wait()
+                rows_ref[i % 2, :, j : j + step] = value
+            if i > 0:
+                finish(i - 1)
+        finish(n - 1)
 
     wide = jax.ShapeDtypeStruct((rows, hidden_units), BF16)
-    messages = jax.ShapeDtypeStruct((n // 2, count, lines, LANES), BF16)
-    return pl.pallas_call(
-        body,
-        grid=(1,),
+    messages = jax.ShapeDtypeStruct((count, lines, LANES), BF16)
+    return pl.pallas_call(
+        body,
         in_specs=[smem_spec()]
-        + [whole(part.shape) for part in grads]
+        + [vmem_spec() for _ in grads]
         + [vmem_spec()] * 4
         + any_specs(2),
-        out_specs=any_specs(1) + [vmem_spec()] * 4,
-        out_shape=[pltpu.HBM((rows, n * width), BF16), wide, wide, messages, messages],
+        out_specs=[vmem_spec()] * (3 + n),
+        out_shape=[jax.ShapeDtypeStruct((rows, n * width), BF16), wide, wide] + [messages] * n,
         scratch_shapes=[
-            pltpu.VMEM((rows, n * width), BF16),
-            pltpu.VMEM((rows, width), F32),
+            pltpu.VMEM((2, rows, width), F32),
             *buffers(6, width, hidden_units),
-            pltpu.SemaphoreType.DMA,
         ],
-        compiler_params=params(32),
+        compiler_params=params(28),
         cost_estimate=cost(
             (4 * n + 2 * (n - early)) * rows * width * hidden_units,
             4 * n * width * hidden_units,
@@ -479,30 +482,30 @@
     )
 
 
-def weight_grad(left, right, name):
+def weight_grads(left, rights, name):
     rows, out_rows = left.shape
-    out_cols = right.shape[1]
+    out_cols = rights[0].shape[1]
+    n = len(rights)
     tile = min(512, out_rows)
     step = min(512, out_cols)
 
-    def body(left_ref, right_ref, out_ref):
-        for j in range(out_cols // step):
-            cols = slice(j * step, (j + 1) * step)
-            out_ref[0, :, cols] = dot(left_ref[...], right_ref[:, cols], 0, 0).astype(BF16)
+    def body(left_ref, *refs):
+        for right_ref, out_ref in zip(refs[:n], refs[n:], strict=True):
+            for j in range(out_cols // step):
+                cols = slice(j * step, (j + 1) * step)
+                out_ref[0, :, cols] = dot(left_ref[...], right_ref[:, cols], 0, 0).astype(BF16)
 
     return pl.pallas_call(
         body,
         grid=(out_rows // tile,),
-        in_specs=[
-            pl.BlockSpec((rows, tile), lambda i: (0, i)),
-            pl.BlockSpec((rows, out_cols), lambda i: (0, 0)),
-        ],
-        out_specs=pl.BlockSpec((1, tile, out_cols), lambda i: (0, i, 0)),
-        out_shape=jax.ShapeDtypeStruct((1, out_rows, out_cols), BF16),
+        in_specs=[pl.BlockSpec((rows, tile), lambda i: (0, i))]
+        + [pl.BlockSpec((rows, out_cols), lambda i: (0, 0))] * n,
+        out_specs=[pl.BlockSpec((1, tile, out_cols), lambda i: (0, i, 0))] * n,
+        out_shape=[jax.ShapeDtypeStruct((1, out_rows, out_cols), BF16)] * n,
         compiler_params=params(32),
-        cost_estimate=cost(4 * rows * out_rows * out_cols, 2 * out_rows * out_cols),
+        cost_estimate=cost(4 * n * rows * out_rows * out_cols, 2 * n * out_rows * out_cols),
         name=name,
-    )(left, right)
+    )(left, *rights)
 
 
 def tie(array, after):
@@ -528,14 +531,11 @@
     return lax.all_to_all(messages, "dp", split_axis=0, concat_axis=0, tiled=True)
 
 
-def gather_parts(own, size, after=None):
-    parts = [own] + [None] * (size - 1)
+def far_parts(own, size, after):
+    parts = []
     for k in range(2, size, 2):
-        parts[k] = across(own, k, size)
-        if after is not None:
-            parts[k] = tie(parts[k], after)
-    for k in range(0, size, 2):
-        parts[k + 1] = across(parts[k], 1, size)
+        part = tie(across(own, k, size), after)
+        parts += [part, across(part, 1, size)]
     return parts
 
 
@@ -554,25 +554,31 @@
 
     early = 2
     token_messages, grad_messages = pack_messages(ids, probs, tokens, grad_out)
-    token_parts = gather_parts(exchange(spread(token_messages)), size)
+    own_tokens = exchange(spread(token_messages))
     own_grads = exchange(spread(grad_messages))
-    first = gate_up_first(index, token_parts[:early], w_gate, w_up, rows, width)
+    near_tokens = [own_tokens, across(own_tokens, 1, size)]
+    first = gate_up_first(index, near_tokens, w_gate, w_up, rows, width)
+    token_parts = near_tokens + far_parts(own_tokens, size, first[0])
     x, hidden, slope, silu = hidden_state(index, token_parts, first, w_gate, w_up, rows, width)
-    grad_parts = gather_parts(tie(own_grads, first[0]), size, slope)
-    grad_early, w_late = early_grads(
-        index, grad_parts[:early], w_down, early, slope, rows, width
-    )
-    y, gate_grad, up_grad, odd, even = input_parts(
+    own_grads = tie(own_grads, first[0])
+    near_grads = [own_grads, across(own_grads, 1, size)]
+    grad_early, w_late = early_grads(index, near_grads, w_down, early, slope, rows, width)
+    grad_parts = near_grads + far_parts(own_grads, size, slope)
+    y, gate_grad, up_grad, *parts = input_parts(
         index, grad_parts, early, grad_early, w_late, slope, silu, w_gate, w_up, rows, width
     )
-    sums = even.astype(F32) + across(odd, 1, size).astype(F32)
+    odd, even = parts[: size // 2], parts[size // 2 :]
+    sums = [
+        here.astype(F32) + across(there, 1, size).astype(F32)
+        for here, there in zip(even, odd, strict=True)
+    ]
+    (grad_down,) = weight_grads(hidden, [y], "down_grad")
     total = sums[-1]
-    for i, k in enumerate(range(size - 2, 0, -2)):
-        total = total + across(sums[i].astype(BF16), k, size).astype(F32)
+    for part, k in zip(sums[:-1], range(size - 2, 0, -2), strict=True):
+        arrived = tie(across(part.astype(BF16), k, size), in_hbm(grad_down))
+        total = total + arrived.astype(F32)
     back = exchange(total.astype(BF16))
-    grad_down = weight_grad(hidden, y, "down_grad")
-    grad_gate = weight_grad(x, gate_grad, "gate_grad")
-    grad_up = weight_grad(x, up_grad, "up_grad")
+    grad_gate, grad_up = weight_grads(in_hbm(x), [gate_grad, up_grad], "gate_up_grads")
     by_slice = back.reshape((EXPERTS, slices) + back.shape[1:]).swapaxes(0, 1)
     input_grad = combine(ids, by_slice, slices, width)
     return (input_grad, grad_gate, grad_up, grad_down)

time: 111 us -> 107 us (0.964)
  Pallas kernels: 66.2 us -> 62.6 us
  local copies, waits for them, and re-layouts: 2.84 us -> 4.19 us
  waiting for transfers between devices: 8.7 us -> 7.42 us
    pallas_call x7 -> x6, Pallas kernels: 62.8 us -> 59.2 us  [the longest x2 26.3 us: weight_grads(): pl.pallas_call(body, grid=(out_rows // tile,), in_specs=[pl.BlockSpec((ro...]
    ppermute x8 -> x9, waiting for transfers between devices: 7.58 us -> 4.25 us  [across(): lax.ppermute(array, 'tensor', [(i, i ^ distance) for i in range(size)])]
    all_to_all x2, waiting for transfers between devices: 1.13 us -> 3.18 us  [exchange(): lax.all_to_all(messages, 'dp', split_axis=0, concat_axis=0, tiled=True)]
    unnamed x16 -> x18, local copies, waits for them, and re-layouts: 2.78 us -> 4.19 us
    ppermute x8 -> x9, starting transfers between devices: 3.6 us -> 3.52 us  [across(): lax.ppermute(array, 'tensor', [(i, i ^ distance) for i in range(size)])]
  transfers between devices with their start and end apart: 10 -> 11, of which waited for: 4 -> 4; matrix products, arithmetic and copies ran while one was open for 0% -> 0% of each run, Pallas kernels for 44% -> 42%
where the time goes in v2:
time: 107 us
  Pallas kernels  62.6 us (59%)
  blocking collectives  19.4 us (18%)
  starting transfers between devices  11.4 us (11%)
  waiting for transfers between devices  7.42 us (7%)
  local copies, waits for them, and re-layouts  4.19 us (4%)
    pallas_call x2, Pallas kernels, weight_grads(): pl.pallas_call(body, grid=(out_rows // tile,), in_specs=[pl.BlockSpec((ro...  26.3 us
    all_to_all x1, blocking collectives, exchange(): lax.all_to_all(messages, 'dp', split_axis=0, concat_axis=0, tiled=True)  19.4 us
    pallas_call x1, Pallas kernels, input_parts(): pl.pallas_call(body, in_specs=[smem_spec()] + [vmem_spec() for _ in grads...  13.8 us
    pallas_call x1, Pallas kernels, hidden_state(): pl.pallas_call(body, in_specs=[smem_spec()] + [vmem_spec() for _ in parts...  7.96 us
    all_to_all x2, starting transfers between devices, exchange(): lax.all_to_all(messages, 'dp', split_axis=0, concat_axis=0, tiled=True)  7.93 us
    pallas_call x1, Pallas kernels, gate_up_first(): pl.pallas_call(body, in_specs=[smem_spec()] + [vmem_spec() for _ in parts...  6.1 us
    pallas_call x1, Pallas kernels, early_grads(): pl.pallas_call(body, in_specs=[smem_spec()] + [vmem_spec() for _ in parts...  5.04 us
    ppermute x9, waiting for transfers between devices, across(): lax.ppermute(array, 'tensor', [(i, i ^ distance) for i in range(size)])  4.25 us
  transfers between devices with their start and end apart: 11, of which 4 were waited for; matrix products, arithmetic and copies ran while one was open for 0% of the time, Pallas kernels for 42%

profile of v2, /device:TPU:0, one launch (start us, length us, event | category | flops | bytes accessed | tf_op | source)
XLA Modules:
  0.0 106.9 jit_solution(13253753482122551735)
XLA Ops:
  0.6 2.3 %pack_messages.1 = (bf16[8,200,128]{2,1,0:T(8,128)(2,1)S(1)}, bf16[8,200,128]{2,1,0:T(8,128)(2,1)}) custom-call(s32[2,128]{1,0:T(2,128)} %bitcast.5, f32[2,128]{1,0:T(2,128)} %bitcast.7, bf16[128,768]{1,0:T(8,128)(2,1)} %tokens_ref.1, bf16[128,768]{1,0:T(8,128)(2,1)} %grads_ref.1), custom_call_target="tpu_custom_call" | custom-call | tf_op jit(solution)/shard_map/pack_messages/pallas_call | solution.py:126
  2.9 19.4 %all_to_all.15.refs_0_ = bf16[8,200,128]{2,1,0:T(8,128)(2,1)S(1)} all-to-all(bf16[8,200,128]{2,1,0:T(8,128)(2,1)S(1)} %get-tuple-element.24), channel_id=1, replica_groups=mesh['dp'=8,'tensor'=4] {'dp'}, dimensions={0} | all-to-all | bytes 819200 | tf_op jit(solution)/shard_map/all_to_all | solution.py:531
  22.4 0.0 collective-permute-start
  22.4 1.5 %collective-permute-start.3 = (bf16[8,200,128]{2,1,0:T(8,128)(2,1)S(1)}, bf16[8,200,128]{2,1,0:T(8,128)(2,1)S(1)}, u32[]{:S(2)}, u32[]{:S(2)}) collective-permute-start(bf16[8,200,128]{2,1,0:T(8,128)(2,1)S(1)} %all_to_all.15.refs_0_), channel_id=1, source_target_pairs={{0,2},{1,3},{2,0},{3,1},{4,6},{5,7},{6,4},{7,5},{8,10},{9,11},{10,... | collective-permute-start | bytes 1228808 | tf_op jit(solution)/shard_map/ppermute | solution.py:527
  23.9 3.5 %all-to-all-start = ((bf16[8,200,128]{2,1,0:T(8,128)(2,1)}), bf16[8,200,128]{2,1,0:T(8,128)(2,1)S(1)}, u32[]{:S(2)}, u32[]{:S(2)}) async-start(bf16[8,200,128]{2,1,0:T(8,128)(2,1)} %get-tuple-element.23), calls=%async_computation | async-start | bytes 819200 | tf_op jit(solution)/shard_map/all_to_all | solution.py:531
  27.3 0.0 collective-permute-done.refs_1_
  27.4 0.0 copy-start.2
  27.4 0.7 copy-done.2
  28.1 0.0 copy-start.3
  28.1 1.0 copy-done.3
  29.1 6.1 %gate_up_first.1 = (f32[264,2048]{1,0:T(8,128)S(1)}, f32[264,2048]{1,0:T(8,128)S(1)}) custom-call(s32[1]{0:T(128)} %bitcast.1.index_ref, bf16[8,200,128]{2,1,0:T(8,128)(2,1)S(1)} %all_to_all.15.refs_0_, bf16[8,200,128]{2,1,0:T(8,128)(2,1)S(1)} %copy-done.3, bf16[1,3072,2048]{2,1,0:T(8,128)(2,1)} %refs_8_.1, bf16[1,3072,2048]{2,1,0:T(8,128)(2,1)} %refs_9_.1), custom_call_target="tpu_custom_call" | custom-call | flops 3321888768 | bytes 12582912 | tf_op jit(solution)/shard_map/gate_up_first/pallas_call | solution.py:274
  35.2 0.0 copy-start
  35.2 0.0 collective-permute-done.3.array_ref
  35.3 1.3 %copy-done = f32[264,2048]{1,0:T(8,128)} copy-done((f32[264,2048]{1,0:T(8,128)}, f32[264,2048]{1,0:T(8,128)S(1)}, u32[]{:S(2)}) %copy-start) | copy-done | bytes 2162712
  36.6 0.2 collective-permute-start.4
  36.8 3.2 %all-to-all-done.array_ref = bf16[8,200,128]{2,1,0:T(8,128)(2,1)S(1)} async-done(((bf16[8,200,128]{2,1,0:T(8,128)(2,1)}), bf16[8,200,128]{2,1,0:T(8,128)(2,1)S(1)}, u32[]{:S(2)}, u32[]{:S(2)}) %all-to-all-start) | async-done | bytes 409632 | tf_op jit(solution)/shard_map/all_to_all | solution.py:531
  40.0 0.0 copy-start.1
  40.0 0.0 copy-start.4
  40.0 0.5 collective-permute-start.2
  40.5 0.0 collective-permute-start.1
  40.5 0.0 collective-permute-done.4.refs_3_
  40.5 1.1 copy-done.1
  41.6 0.0 copy-done.4
  41.6 8.0 %hidden_state.1 = (bf16[264,3072]{1,0:T(8,128)(2,1)S(1)}, bf16[264,2048]{1,0:T(8,128)(2,1)S(1)}, bf16[264,2048]{1,0:T(8,128)(2,1)S(1)}, bf16[264,2048]{1,0:T(8,128)(2,1)S(1)}) custom-call(s32[1]{0:T(128)} %bitcast.1.index_ref, bf16[8,200,128]{2,1,0:T(8,128)(2,1)S(1)} %all_to_all.15.refs_0_, bf16[8,200,128]{2,1,0:T(8,128)(2,1)S(1)} %copy-done.4, ...), custom_call_target="tpu_custom_call" | custom-call | flops 3321888768 | bytes 12582912 | tf_op jit(solution)/shard_map/hidden_state/pallas_call | solution.py:329
  49.6 0.0 copy-start.6
  49.6 0.9 collective-permute-done.2.array_ref
  50.5 0.0 collective-permute-start.5
  50.5 0.0 collective-permute-done.1.refs_1_
  50.5 5.0 %early_grads.1 = (f32[264,2048]{1,0:T(8,128)S(1)}, bf16[2,2048,768]{2,1,0:T(8,128)(2,1)S(1)}) custom-call(s32[1]{0:T(128)} %bitcast.1.index_ref, bf16[8,200,128]{2,1,0:T(8,128)(2,1)S(1)} %tie.4.refs_0_, bf16[8,200,128]{2,1,0:T(8,128)(2,1)S(1)} %collective-permute-done.1.refs_1_, bf16[1,2048,3072]{2,1,0:T(8,128)(2,1)} %refs_2_.3, ...), custom_call_target="tpu_custom_call" | custom-call | flops 1660944384 | bytes 12582912 | tf_op jit(solution)/shard_map/early_grads/pallas_call | solution.py:390
  55.6 0.0 copy-done.6
  55.6 0.0 collective-permute-done.5.refs_3_
  55.6 13.8 %input_parts.1 = (bf16[264,3072]{1,0:T(8,128)(2,1)S(1)}, bf16[264,2048]{1,0:T(8,128)(2,1)S(1)}, bf16[264,2048]{1,0:T(8,128)(2,1)S(1)}, bf16[8,200,128]{2,1,0:T(8...) custom-call(s32[1]{0:T(128)} %bitcast.1.index_ref, ...), custom_call_target="tpu_custom_call" | custom-call | flops 8304721920 | bytes 25165824 | tf_op jit(solution)/shard_map/input_parts/pallas_call | solution.py:455
  69.4 0.0 copy-start.7
  69.4 0.6 collective-permute-start.7
  70.0 0.1 collective-permute-start.6
  70.0 1.3 %collective-permute-done.7 = bf16[8,200,128]{2,1,0:T(8,128)(2,1)S(1)} collective-permute-done((bf16[8,200,128]{2,1,0:T(8,128)(2,1)S(1)}, bf16[8,200,128]{2,1,0:T(8,128)(2,1)S(1)}, u32[]{:S(2)}, u32[]{:S(2)}) %collective-permute-start.7) | collective-permute-done | bytes 409632 | tf_op jit(solution)/shard_map/ppermute | solution.py:527
  71.3 0.1 add_convert_fusion.1
  71.5 0.6 collective-permute-start.8
  72.1 9.2 %down_grad.1.after_ref = bf16[1,2048,3072]{2,1,0:T(8,128)(2,1)} custom-call(bf16[264,2048]{1,0:T(8,128)(2,1)S(1)} %get-tuple-element.35.left_ref, bf16[264,3072]{1,0:T(8,128)(2,1)S(1)} %get-tuple-element.36.refs_0_), custom_call_target="tpu_custom_call" | custom-call | flops 6643777536 | bytes 12582912 | tf_op jit(solution)/shard_map/down_grad/pallas_call | solution.py:498
  81.3 0.0 copy-done.7
  81.3 2.0 %collective-permute-done.8.array_ref = bf16[8,200,128]{2,1,0:T(8,128)(2,1)S(1)} collective-permute-done((bf16[8,200,128]{2,1,0:T(8,128)(2,1)S(1)}, bf16[8,200,128]{2,1,0:T(8,128)(2,1)S(1)}, u32[]{:S(2)}, u32[]{:S(2)}) %collective-permute-start.8) | collective-permute-done | bytes 409632 | tf_op jit(solution)/shard_map/ppermute | solution.py:527
  83.3 0.0 copy-start.8
  83.3 0.0 collective-permute-done.6
  83.3 0.9 add_convert_fusion
  84.2 4.5 %all-to-all-start.2 = ((bf16[8,200,128]{2,1,0:T(8,128)(2,1)}), bf16[8,200,128]{2,1,0:T(8,128)(2,1)S(1)}, u32[]{:S(2)}, u32[]{:S(2)}) async-start(bf16[8,200,128]{2,1,0:T(8,128)(2,1)} %add_convert_fusion), calls=%async_computation.2 | async-start | bytes 819200 | tf_op jit(solution)/shard_map/all_to_all | solution.py:531
  88.7 0.0 copy-done.8
  88.7 0.0 copy-start.5
  88.7 17.1 %gate_up_grads.1 = (bf16[1,3072,2048]{2,1,0:T(8,128)(2,1)}, bf16[1,3072,2048]{2,1,0:T(8,128)(2,1)}) custom-call(bf16[264,3072]{1,0:T(8,128)(2,1)} %copy-done.6, bf16[264,2048]{1,0:T(8,128)(2,1)S(1)} %get-tuple-element.38.refs_0_, bf16[264,2048]{1,0:T(8,128)(2,1)S(1)} %copy-done.8), custom_call_target="tpu_custom_call" | custom-call | flops 13287555072 | bytes 25165824 | tf_op jit(solution)/shard_map/gate_up_grads/pallas_call | solution.py:498
  105.8 0.0 all-to-all-done.2
  105.8 0.0 copy-done.5
  105.8 1.1 %combine.1 = bf16[128,768]{1,0:T(8,128)(2,1)} custom-call(s32[2,128]{1,0:T(2,128)S(1)} %bitcast.6, bf16[1,8,200,128]{3,2,1,0:T(8,128)(2,1)S(1)} %bitcast.4), custom_call_target="tpu_custom_call" | custom-call | tf_op jit(solution)/shard_map/combine/pallas_call | solution.py:148
  (4 shorter events, 0.0 us)
Async XLA Ops:
  22.4 5.0 %collective-permute-start = (bf16[8,200,128]{2,1,0:T(8,128)(2,1)S(1)}, bf16[8,200,128]{2,1,0:T(8,128)(2,1)S(1)}, u32[]{:S(2)}, u32[]{:S(2)}) collective-permute-start(bf16[8,200,128]{2,1,0:T(8,128)(2,1)S(1)} %all_to_all.15.refs_0_), channel_id=1, source_target_pairs={{0,1},{1,0},{2,3},{3,2},{4,5},{5,4},{6,7},{7,6},{8,9},{9,8},{10,11... | collective-permute-start | bytes 1228808 | tf_op jit(solution)/shard_map/ppermute | solution.py:527
  22.4 12.8 %collective-permute-start.3 = (bf16[8,200,128]{2,1,0:T(8,128)(2,1)S(1)}, bf16[8,200,128]{2,1,0:T(8,128)(2,1)S(1)}, u32[]{:S(2)}, u32[]{:S(2)}) collective-permute-start(bf16[8,200,128]{2,1,0:T(8,128)(2,1)S(1)} %all_to_all.15.refs_0_), channel_id=1, source_target_pairs={{0,2},{1,3},{2,0},{3,1},{4,6},{5,7},{6,4},{7,5},{8,10},{9,11},{10,... | collective-permute-start | bytes 1228808 | tf_op jit(solution)/shard_map/ppermute | solution.py:527
  23.9 16.1 %all-to-all-start = ((bf16[8,200,128]{2,1,0:T(8,128)(2,1)}), bf16[8,200,128]{2,1,0:T(8,128)(2,1)S(1)}, u32[]{:S(2)}, u32[]{:S(2)}) async-start(bf16[8,200,128]{2,1,0:T(8,128)(2,1)} %get-tuple-element.23), calls=%async_computation | async-start | bytes 819200 | tf_op jit(solution)/shard_map/all_to_all | solution.py:531
  27.4 0.8 copy-start.2
  28.1 1.0 copy-start.3
  35.2 1.3 %copy-start = (f32[264,2048]{1,0:T(8,128)}, f32[264,2048]{1,0:T(8,128)S(1)}, u32[]{:S(2)}) copy-start(f32[264,2048]{1,0:T(8,128)S(1)} %get-tuple-element.26.refs_5_) | copy-start | bytes 6488068
  36.6 3.9 %collective-permute-start.4 = (bf16[8,200,128]{2,1,0:T(8,128)(2,1)S(1)}, bf16[8,200,128]{2,1,0:T(8,128)(2,1)}, u32[]{:S(2)}, u32[]{:S(2)}) collective-permute-start(bf16[8,200,128]{2,1,0:T(8,128)(2,1)S(1)} %tie.5.refs_2_), channel_id=1, source_target_pairs={{0,1},{1,0},{2,3},{3,2},{4,5},{5,4},{6,7},{7,6},{8,9},{9,8},{10,11... | collective-permute-start | bytes 1228808 | tf_op jit(solution)/shard_map/ppermute | solution.py:527
  40.0 1.6 %copy-start.1 = (f32[264,2048]{1,0:T(8,128)S(1)}, f32[264,2048]{1,0:T(8,128)}, u32[]{:S(2)}) copy-start(f32[264,2048]{1,0:T(8,128)} %copy-done) | copy-start | bytes 6488068
  40.0 1.6 %copy-start.4 = (bf16[8,200,128]{2,1,0:T(8,128)(2,1)S(1)}, bf16[8,200,128]{2,1,0:T(8,128)(2,1)}, u32[]{:S(2)}) copy-start(bf16[8,200,128]{2,1,0:T(8,128)(2,1)} %copy-done.2) | copy-start | bytes 1228804
  40.0 10.6 %collective-permute-start.2 = (bf16[8,200,128]{2,1,0:T(8,128)(2,1)S(1)}, bf16[8,200,128]{2,1,0:T(8,128)(2,1)S(1)}, u32[]{:S(2)}, u32[]{:S(2)}) collective-permute-start(bf16[8,200,128]{2,1,0:T(8,128)(2,1)S(1)} %tie.4.refs_0_), channel_id=1, source_target_pairs={{0,2},{1,3},{2,0},{3,1},{4,6},{5,7},{6,4},{7,5},{8,10},{9,11},{10,... | collective-permute-start | bytes 1228808 | tf_op jit(solution)/shard_map/ppermute | solution.py:527
  40.5 10.0 %collective-permute-start.1 = (bf16[8,200,128]{2,1,0:T(8,128)(2,1)S(1)}, bf16[8,200,128]{2,1,0:T(8,128)(2,1)S(1)}, u32[]{:S(2)}, u32[]{:S(2)}) collective-permute-start(bf16[8,200,128]{2,1,0:T(8,128)(2,1)S(1)} %tie.4.refs_0_), channel_id=1, source_target_pairs={{0,1},{1,0},{2,3},{3,2},{4,5},{5,4},{6,7},{7,6},{8,9},{9,8},{10,11... | collective-permute-start | bytes 1228808 | tf_op jit(solution)/shard_map/ppermute | solution.py:527
  49.6 6.0 %copy-start.6 = (bf16[264,3072]{1,0:T(8,128)(2,1)}, bf16[264,3072]{1,0:T(8,128)(2,1)S(1)}, u32[]{:S(2)}) copy-start(bf16[264,3072]{1,0:T(8,128)(2,1)S(1)} %get-tuple-element.37.left_ref) | copy-start | bytes 4866052
  50.5 5.1 %collective-permute-start.5 = (bf16[8,200,128]{2,1,0:T(8,128)(2,1)S(1)}, bf16[8,200,128]{2,1,0:T(8,128)(2,1)S(1)}, u32[]{:S(2)}, u32[]{:S(2)}) collective-permute-start(bf16[8,200,128]{2,1,0:T(8,128)(2,1)S(1)} %tie.6.refs_2_), channel_id=1, source_target_pairs={{0,1},{1,0},{2,3},{3,2},{4,5},{5,4},{6,7},{7,6},{8,9},{9,8},{10,11... | collective-permute-start | bytes 1228808 | tf_op jit(solution)/shard_map/ppermute | solution.py:527
  69.4 11.9 %copy-start.7 = (bf16[264,2048]{1,0:T(8,128)(2,1)}, bf16[264,2048]{1,0:T(8,128)(2,1)S(1)}, u32[]{:S(2)}) copy-start(bf16[264,2048]{1,0:T(8,128)(2,1)S(1)} %get-tuple-element.39.refs_1_) | copy-start | bytes 3244036
  69.4 1.9 %collective-permute-start.7 = (bf16[8,200,128]{2,1,0:T(8,128)(2,1)S(1)}, bf16[8,200,128]{2,1,0:T(8,128)(2,1)S(1)}, u32[]{:S(2)}, u32[]{:S(2)}) collective-permute-start(bf16[8,200,128]{2,1,0:T(8,128)(2,1)S(1)} %get-tuple-element.34), channel_id=1, source_target_pairs={{0,1},{1,0},{2,3},{3,2},{4,5},{5,4},{6,7},{7,6},{8,9},{9,8},{10,11... | collective-permute-start | bytes 1228808 | tf_op jit(solution)/shard_map/ppermute | solution.py:527
  70.0 13.3 %collective-permute-start.6 = (bf16[8,200,128]{2,1,0:T(8,128)(2,1)S(1)}, bf16[8,200,128]{2,1,0:T(8,128)(2,1)S(1)}, u32[]{:S(2)}, u32[]{:S(2)}) collective-permute-start(bf16[8,200,128]{2,1,0:T(8,128)(2,1)S(1)} %get-tuple-element.32), channel_id=1, source_target_pairs={{0,1},{1,0},{2,3},{3,2},{4,5},{5,4},{6,7},{7,6},{8,9},{9,8},{10,11... | collective-permute-start | bytes 1228808 | tf_op jit(solution)/shard_map/ppermute | solution.py:527
  71.5 11.8 %collective-permute-start.8 = (bf16[8,200,128]{2,1,0:T(8,128)(2,1)S(1)}, bf16[8,200,128]{2,1,0:T(8,128)(2,1)S(1)}, u32[]{:S(2)}, u32[]{:S(2)}) collective-permute-start(bf16[8,200,128]{2,1,0:T(8,128)(2,1)S(1)} %add_convert_fusion.1), channel_id=1, source_target_pairs={{0,2},{1,3},{2,0},{3,1},{4,6},{5,7},{6,4},{7,5},{8,10},{9,11},{10,... | collective-permute-start | bytes 1228808 | tf_op jit(solution)/shard_map/ppermute | solution.py:527
  83.3 5.4 %copy-start.8 = (bf16[264,2048]{1,0:T(8,128)(2,1)S(1)}, bf16[264,2048]{1,0:T(8,128)(2,1)}, u32[]{:S(2)}) copy-start(bf16[264,2048]{1,0:T(8,128)(2,1)} %copy-done.7) | copy-start | bytes 3244036
  84.2 21.6 %all-to-all-start.2 = ((bf16[8,200,128]{2,1,0:T(8,128)(2,1)}), bf16[8,200,128]{2,1,0:T(8,128)(2,1)S(1)}, u32[]{:S(2)}, u32[]{:S(2)}) async-start(bf16[8,200,128]{2,1,0:T(8,128)(2,1)} %add_convert_fusion), calls=%async_computation.2 | async-start | bytes 819200 | tf_op jit(solution)/shard_map/all_to_all | solution.py:531
  88.7 17.1 %copy-start.5 = (s32[128,2]{0,1:T(2,128)S(1)}, s32[128,2]{0,1:T(2,128)}, u32[]{:S(2)}) copy-start(s32[128,2]{0,1:T(2,128)} %param.9) | copy-start | bytes 3076

commit v3 on v2

--- a/solution.py
+++ b/solution.py
@@ -112,25 +112,41 @@
     return pltpu.with_memory_space_constraint(array, pltpu.HBM)
 
 
-def pack_messages(ids, probs, tokens, grads):
-    def body(ids_ref, probs_ref, tokens_ref, grads_ref, token_out, grad_out):
+def pack_tokens(ids, tokens):
+    def body(ids_ref, tokens_ref, out_ref):
+        picks = select_rows(ids_ref[...])
+        pack(out_ref, dot(picks.astype(BF16), tokens_ref[...], 1, 0))
+
+    shape = (EXPERTS, message_rows(tokens.shape[1]), LANES)
+    arrays = (ids, tokens)
+    return pl.pallas_call(
+        body,
+        grid=(1,),
+        in_specs=[whole(array.shape) for array in arrays],
+        out_specs=whole(shape),
+        out_shape=jax.ShapeDtypeStruct(shape, BF16),
+        compiler_params=params(8),
+        name="pack_tokens",
+    )(*[in_hbm(array) for array in arrays])
+
+
+def pack_grads(ids, probs, grads):
+    def body(ids_ref, probs_ref, grads_ref, out_ref):
         ids_in = ids_ref[...]
         picks = select_rows(ids_in)
         scale = row_weights(ids_in, probs_ref[...], picks)
-        picks = picks.astype(BF16)
-        pack(token_out, dot(picks, tokens_ref[...], 1, 0))
-        pack(grad_out, dot(picks, grads_ref[...], 1, 0) * scale)
+        pack(out_ref, dot(picks.astype(BF16), grads_ref[...], 1, 0) * scale)
 
     shape = (EXPERTS, message_rows(grads.shape[1]), LANES)
-    arrays = (ids, probs, tokens, grads)
+    arrays = (ids, probs, grads)
     return pl.pallas_call(
         body,
         grid=(1,),
         in_specs=[whole(array.shape) for array in arrays],
-        out_specs=[whole(shape)] * 2,
-        out_shape=[jax.ShapeDtypeStruct(shape, BF16)] * 2,
+        out_specs=whole(shape),
+        out_shape=jax.ShapeDtypeStruct(shape, BF16),
         compiler_params=params(8),
-        name="pack_messages",
+        name="pack_grads",
     )(*[in_hbm(array) for array in arrays])
 
 
@@ -553,8 +569,8 @@
         return messages if slices == 1 else jnp.repeat(messages, slices, axis=0)
 
     early = 2
-    token_messages, grad_messages = pack_messages(ids, probs, tokens, grad_out)
-    own_tokens = exchange(spread(token_messages))
+    grad_messages = pack_grads(ids, probs, grad_out)
+    own_tokens = tie(exchange(spread(pack_tokens(ids, tokens))), grad_messages)
     own_grads = exchange(spread(grad_messages))
     near_tokens = [own_tokens, across(own_tokens, 1, size)]
     first = gate_up_first(index, near_tokens, w_gate, w_up, rows, width)
@@ -572,13 +588,13 @@
         here.astype(F32) + across(there, 1, size).astype(F32)
         for here, there in zip(even, odd, strict=True)
     ]
-    (grad_down,) = weight_grads(hidden, [y], "down_grad")
+    grad_gate, grad_up = weight_grads(x, [gate_grad, up_grad], "gate_up_grads")
     total = sums[-1]
     for part, k in zip(sums[:-1], range(size - 2, 0, -2), strict=True):
-        arrived = tie(across(part.astype(BF16), k, size), in_hbm(grad_down))
+        arrived = tie(across(part.astype(BF16), k, size), in_hbm(grad_gate))
         total = total + arrived.astype(F32)
     back = exchange(total.astype(BF16))
-    grad_gate, grad_up = weight_grads(in_hbm(x), [gate_grad, up_grad], "gate_up_grads")
+    (grad_down,) = weight_grads(in_hbm(hidden), [y], "down_grad")
     by_slice = back.reshape((EXPERTS, slices) + back.shape[1:]).swapaxes(0, 1)
     input_grad = combine(ids, by_slice, slices, width)
     return (input_grad, grad_gate, grad_up, grad_down)

time: 107 us -> 107 us (level)
  blocking collectives: 19.4 us -> 0 us
  waiting for transfers between devices: 7.42 us -> 17.5 us
  starting transfers between devices: 11.4 us -> 18.8 us
  Pallas kernels: 62.6 us -> 64.5 us
    all_to_all x1 -> x0, blocking collectives: 19.4 us -> none  [exchange(): lax.all_to_all(messages, 'dp', split_axis=0, concat_axis=0, tiled=True)]
    all_to_all x2 -> x3, waiting for transfers between devices: 3.18 us -> 15.3 us  [exchange(): lax.all_to_all(messages, 'dp', split_axis=0, concat_axis=0, tiled=True)]
    all_to_all x2 -> x3, starting transfers between devices: 7.93 us -> 15.4 us  [exchange(): lax.all_to_all(messages, 'dp', split_axis=0, concat_axis=0, tiled=True)]
    ppermute x9, waiting for transfers between devices: 4.25 us -> 2.18 us  [across(): lax.ppermute(array, 'tensor', [(i, i ^ distance) for i in range(size)])]
    pallas_call x1 -> x2, Pallas kernels: 2.31 us -> 4.19 us  [the longest x1 2.1 us: pack_grads(): pl.pallas_call(body, grid=(1,), in_specs=[whole(array.shape) for array in...]
    unnamed x18 -> x14, local copies, waits for them, and re-layouts: 4.19 us -> 4.18 us
  transfers between devices with their start and end apart: 11 -> 12, of which waited for: 4 -> 5; matrix products, arithmetic and copies ran while one was open for 0% -> 0% of each run, Pallas kernels for 42% -> 45%
where the time goes in v3:
time: 107 us
  Pallas kernels  64.5 us (60%)
  starting transfers between devices  18.8 us (18%)
  waiting for transfers between devices  17.5 us (16%)
  local copies, waits for them, and re-layouts  4.18 us (4%)
    pallas_call x2, Pallas kernels, weight_grads(): pl.pallas_call(body, grid=(out_rows // tile,), in_specs=[pl.BlockSpec((ro...  26.4 us
    all_to_all x3, starting transfers between devices, exchange(): lax.all_to_all(messages, 'dp', split_axis=0, concat_axis=0, tiled=True)  15.4 us
    all_to_all x3, waiting for transfers between devices, exchange(): lax.all_to_all(messages, 'dp', split_axis=0, concat_axis=0, tiled=True)  15.3 us
    pallas_call x1, Pallas kernels, input_parts(): pl.pallas_call(body, in_specs=[smem_spec()] + [vmem_spec() for _ in grads...  13.8 us
    pallas_call x1, Pallas kernels, hidden_state(): pl.pallas_call(body, in_specs=[smem_spec()] + [vmem_spec() for _ in parts...  7.96 us
    pallas_call x1, Pallas kernels, gate_up_first(): pl.pallas_call(body, in_specs=[smem_spec()] + [vmem_spec() for _ in parts...  6.1 us
    pallas_call x1, Pallas kernels, early_grads(): pl.pallas_call(body, in_specs=[smem_spec()] + [vmem_spec() for _ in parts...  5.04 us
    unnamed x14, local copies, waits for them, and re-layouts  4.18 us
  transfers between devices with their start and end apart: 12, of which 5 were waited for; matrix products, arithmetic and copies ran while one was open for 0% of the time, Pallas kernels for 45%

profile of v3, /device:TPU:0, one launch (start us, length us, event | category | flops | bytes accessed | tf_op | source)
XLA Modules:
  0.0 106.7 jit_solution(6544640549802224503)
XLA Ops:
  0.6 2.1 %pack_tokens.1 = bf16[8,200,128]{2,1,0:T(8,128)(2,1)} custom-call(s32[2,128]{1,0:T(2,128)} %bitcast.5, bf16[128,768]{1,0:T(8,128)(2,1)} %tokens_ref.1), custom_call_target="tpu_custom_call" | custom-call | tf_op jit(solution)/shard_map/pack_tokens/pallas_call | solution.py:122
  2.7 7.3 %all-to-all-start.1 = ((bf16[8,200,128]{2,1,0:T(8,128)(2,1)}), bf16[8,200,128]{2,1,0:T(8,128)(2,1)S(1)}, u32[]{:S(2)}, u32[]{:S(2)}) async-start(bf16[8,200,128]{2,1,0:T(8,128)(2,1)} %pack_tokens.1), calls=%async_computation.1 | async-start | bytes 819200 | tf_op jit(solution)/shard_map/all_to_all | solution.py:547
  10.0 2.1 %pack_grads.1.after_ref = bf16[8,200,128]{2,1,0:T(8,128)(2,1)} custom-call(s32[2,128]{1,0:T(2,128)} %bitcast.6, f32[2,128]{1,0:T(2,128)} %bitcast.8, bf16[128,768]{1,0:T(8,128)(2,1)} %grads_ref.1), custom_call_target="tpu_custom_call" | custom-call | tf_op jit(solution)/shard_map/pack_grads/pallas_call | solution.py:142
  12.1 9.9 %all-to-all-done.1.array_ref = bf16[8,200,128]{2,1,0:T(8,128)(2,1)S(1)} async-done(((bf16[8,200,128]{2,1,0:T(8,128)(2,1)}), bf16[8,200,128]{2,1,0:T(8,128)(2,1)S(1)}, u32[]{:S(2)}, u32[]{:S(2)}) %all-to-all-start.1) | async-done | bytes 409632 | tf_op jit(solution)/shard_map/all_to_all | solution.py:547
  22.0 0.0 collective-permute-start
  22.0 1.5 %collective-permute-start.3 = (bf16[8,200,128]{2,1,0:T(8,128)(2,1)S(1)}, bf16[8,200,128]{2,1,0:T(8,128)(2,1)S(1)}, u32[]{:S(2)}, u32[]{:S(2)}) collective-permute-start(bf16[8,200,128]{2,1,0:T(8,128)(2,1)S(1)} %tie.5.refs_0_), channel_id=1, source_target_pairs={{0,2},{1,3},{2,0},{3,1},{4,6},{5,7},{6,4},{7,5},{8,10},{9,11},{10,... | collective-permute-start | bytes 1228808 | tf_op jit(solution)/shard_map/ppermute | solution.py:543
  23.5 3.6 %all-to-all-start = ((bf16[8,200,128]{2,1,0:T(8,128)(2,1)}), bf16[8,200,128]{2,1,0:T(8,128)(2,1)S(1)}, u32[]{:S(2)}, u32[]{:S(2)}) async-start(bf16[8,200,128]{2,1,0:T(8,128)(2,1)} %pack_grads.1.after_ref), calls=%async_computation | async-start | bytes 819200 | tf_op jit(solution)/shard_map/all_to_all | solution.py:547
  27.2 0.0 collective-permute-done.refs_1_
  27.2 0.0 copy-start.2
  27.2 0.7 copy-done.2
  27.9 0.0 copy-start.3
  27.9 1.0 copy-done.3
  28.9 6.1 %gate_up_first.1 = (f32[264,2048]{1,0:T(8,128)S(1)}, f32[264,2048]{1,0:T(8,128)S(1)}) custom-call(s32[1]{0:T(128)} %bitcast.1.index_ref, bf16[8,200,128]{2,1,0:T(8,128)(2,1)S(1)} %tie.5.refs_0_, bf16[8,200,128]{2,1,0:T(8,128)(2,1)S(1)} %copy-done.3, bf16[1,3072,2048]{2,1,0:T(8,128)(2,1)} %refs_8_.1, bf16[1,3072,2048]{2,1,0:T(8,128)(2,1)} %refs_9_.1), custom_call_target="tpu_custom_call" | custom-call | flops 3321888768 | bytes 12582912 | tf_op jit(solution)/shard_map/gate_up_first/pallas_call | solution.py:290
  35.0 0.0 copy-start
  35.0 0.0 collective-permute-done.3.array_ref
  35.1 1.3 %copy-done = f32[264,2048]{1,0:T(8,128)} copy-done((f32[264,2048]{1,0:T(8,128)}, f32[264,2048]{1,0:T(8,128)S(1)}, u32[]{:S(2)}) %copy-start) | copy-done | bytes 2162712
  36.4 0.1 collective-permute-start.4
  36.4 3.2 %all-to-all-done.array_ref = bf16[8,200,128]{2,1,0:T(8,128)(2,1)S(1)} async-done(((bf16[8,200,128]{2,1,0:T(8,128)(2,1)}), bf16[8,200,128]{2,1,0:T(8,128)(2,1)S(1)}, u32[]{:S(2)}, u32[]{:S(2)}) %all-to-all-start) | async-done | bytes 409632 | tf_op jit(solution)/shard_map/all_to_all | solution.py:547
  39.6 0.0 copy-start.1
  39.6 0.0 copy-start.4
  39.6 0.5 collective-permute-start.2
  40.1 0.0 collective-permute-start.1
  40.2 0.0 collective-permute-done.4.refs_3_
  40.2 1.1 copy-done.1
  41.2 0.0 copy-done.4
  41.3 8.0 %hidden_state.1 = (bf16[264,3072]{1,0:T(8,128)(2,1)S(1)}, bf16[264,2048]{1,0:T(8,128)(2,1)S(1)}, bf16[264,2048]{1,0:T(8,128)(2,1)S(1)}, bf16[264,2048]{1,0:T(8,128)(2,1)S(1)}) custom-call(s32[1]{0:T(128)} %bitcast.1.index_ref, bf16[8,200,128]{2,1,0:T(8,128)(2,1)S(1)} %tie.5.refs_0_, bf16[8,200,128]{2,1,0:T(8,128)(2,1)S(1)} %copy-done.4, ...), custom_call_target="tpu_custom_call" | custom-call | flops 3321888768 | bytes 12582912 | tf_op jit(solution)/shard_map/hidden_state/pallas_call | solution.py:345
  49.2 0.0 copy-start.6
  49.2 0.9 collective-permute-done.2.array_ref
  50.1 0.0 collective-permute-start.5
  50.1 0.0 collective-permute-done.1.refs_1_
  50.1 5.0 %early_grads.1 = (f32[264,2048]{1,0:T(8,128)S(1)}, bf16[2,2048,768]{2,1,0:T(8,128)(2,1)S(1)}) custom-call(s32[1]{0:T(128)} %bitcast.1.index_ref, bf16[8,200,128]{2,1,0:T(8,128)(2,1)S(1)} %tie.6.refs_0_, bf16[8,200,128]{2,1,0:T(8,128)(2,1)S(1)} %collective-permute-done.1.refs_1_, bf16[1,2048,3072]{2,1,0:T(8,128)(2,1)} %refs_2_.3, ...), custom_call_target="tpu_custom_call" | custom-call | flops 1660944384 | bytes 12582912 | tf_op jit(solution)/shard_map/early_grads/pallas_call | solution.py:406
  55.2 0.0 copy-done.6
  55.2 0.0 collective-permute-done.5.refs_3_
  55.2 13.8 %input_parts.1 = (bf16[264,3072]{1,0:T(8,128)(2,1)S(1)}, bf16[264,2048]{1,0:T(8,128)(2,1)S(1)}, bf16[264,2048]{1,0:T(8,128)(2,1)S(1)}, bf16[8,200,128]{2,1,0:T(8...) custom-call(s32[1]{0:T(128)} %bitcast.1.index_ref, ...), custom_call_target="tpu_custom_call" | custom-call | flops 8304721920 | bytes 25165824 | tf_op jit(solution)/shard_map/input_parts/pallas_call | solution.py:471
  69.0 0.6 collective-permute-start.7
  69.5 0.1 collective-permute-start.6
  69.6 1.3 %collective-permute-done.7 = bf16[8,200,128]{2,1,0:T(8,128)(2,1)S(1)} collective-permute-done((bf16[8,200,128]{2,1,0:T(8,128)(2,1)S(1)}, bf16[8,200,128]{2,1,0:T(8,128)(2,1)S(1)}, u32[]{:S(2)}, u32[]{:S(2)}) %collective-permute-start.7) | collective-permute-done | bytes 409632 | tf_op jit(solution)/shard_map/ppermute | solution.py:543
  70.9 0.1 add_convert_fusion.1
  71.0 0.6 collective-permute-start.8
  71.6 16.3 %gate_up_grads.1 = (bf16[1,3072,2048]{2,1,0:T(8,128)(2,1)}, bf16[1,3072,2048]{2,1,0:T(8,128)(2,1)}) custom-call(bf16[264,3072]{1,0:T(8,128)(2,1)S(1)} %get-tuple-element.31.left_ref, bf16[264,2048]{1,0:T(8,128)(2,1)S(1)} %get-tuple-element.32.refs_0_, bf16[264,2048]{1,0:T(8,128)(2,1)S(1)} %get-tuple-element.33.refs_1_), custom_call_target="tpu_custom_call" | custom-call | flops 13287555072 | bytes 25165824 | tf_op jit(solution)/shard_map/gate_up_grads/pallas_call | solution.py:514
  87.9 0.0 collective-permute-done.8.array_ref
  87.9 0.0 collective-permute-done.6
  87.9 0.9 add_convert_fusion
  88.8 4.5 %all-to-all-start.2 = ((bf16[8,200,128]{2,1,0:T(8,128)(2,1)}), bf16[8,200,128]{2,1,0:T(8,128)(2,1)S(1)}, u32[]{:S(2)}, u32[]{:S(2)}) async-start(bf16[8,200,128]{2,1,0:T(8,128)(2,1)} %add_convert_fusion), calls=%async_computation.2 | async-start | bytes 819200 | tf_op jit(solution)/shard_map/all_to_all | solution.py:547
  93.3 0.0 copy-start.5
  93.3 10.1 %down_grad.1 = bf16[1,2048,3072]{2,1,0:T(8,128)(2,1)} custom-call(bf16[264,2048]{1,0:T(8,128)(2,1)} %copy-done.6, bf16[264,3072]{1,0:T(8,128)(2,1)S(1)} %get-tuple-element.37.refs_0_), custom_call_target="tpu_custom_call" | custom-call | flops 6643777536 | bytes 12582912 | tf_op jit(solution)/shard_map/down_grad/pallas_call | solution.py:514
  103.4 2.2 %all-to-all-done.2 = bf16[8,200,128]{2,1,0:T(8,128)(2,1)S(1)} async-done(((bf16[8,200,128]{2,1,0:T(8,128)(2,1)}), bf16[8,200,128]{2,1,0:T(8,128)(2,1)S(1)}, u32[]{:S(2)}, u32[]{:S(2)}) %all-to-all-start.2) | async-done | bytes 409632 | tf_op jit(solution)/shard_map/all_to_all | solution.py:547
  105.6 0.0 copy-done.5
  105.6 1.1 %combine.1 = bf16[128,768]{1,0:T(8,128)(2,1)} custom-call(s32[2,128]{1,0:T(2,128)S(1)} %bitcast.7, bf16[1,8,200,128]{3,2,1,0:T(8,128)(2,1)S(1)} %bitcast.4), custom_call_target="tpu_custom_call" | custom-call | tf_op jit(solution)/shard_map/combine/pallas_call | solution.py:164
  (5 shorter events, 0.0 us)
Async XLA Ops:
  2.7 19.3 %all-to-all-start.1 = ((bf16[8,200,128]{2,1,0:T(8,128)(2,1)}), bf16[8,200,128]{2,1,0:T(8,128)(2,1)S(1)}, u32[]{:S(2)}, u32[]{:S(2)}) async-start(bf16[8,200,128]{2,1,0:T(8,128)(2,1)} %pack_tokens.1), calls=%async_computation.1 | async-start | bytes 819200 | tf_op jit(solution)/shard_map/all_to_all | solution.py:547
  22.0 5.1 %collective-permute-start = (bf16[8,200,128]{2,1,0:T(8,128)(2,1)S(1)}, bf16[8,200,128]{2,1,0:T(8,128)(2,1)S(1)}, u32[]{:S(2)}, u32[]{:S(2)}) collective-permute-start(bf16[8,200,128]{2,1,0:T(8,128)(2,1)S(1)} %tie.5.refs_0_), channel_id=1, source_target_pairs={{0,1},{1,0},{2,3},{3,2},{4,5},{5,4},{6,7},{7,6},{8,9},{9,8},{10,11... | collective-permute-start | bytes 1228808 | tf_op jit(solution)/shard_map/ppermute | solution.py:543
  22.0 13.0 %collective-permute-start.3 = (bf16[8,200,128]{2,1,0:T(8,128)(2,1)S(1)}, bf16[8,200,128]{2,1,0:T(8,128)(2,1)S(1)}, u32[]{:S(2)}, u32[]{:S(2)}) collective-permute-start(bf16[8,200,128]{2,1,0:T(8,128)(2,1)S(1)} %tie.5.refs_0_), channel_id=1, source_target_pairs={{0,2},{1,3},{2,0},{3,1},{4,6},{5,7},{6,4},{7,5},{8,10},{9,11},{10,... | collective-permute-start | bytes 1228808 | tf_op jit(solution)/shard_map/ppermute | solution.py:543
  23.5 16.1 %all-to-all-start = ((bf16[8,200,128]{2,1,0:T(8,128)(2,1)}), bf16[8,200,128]{2,1,0:T(8,128)(2,1)S(1)}, u32[]{:S(2)}, u32[]{:S(2)}) async-start(bf16[8,200,128]{2,1,0:T(8,128)(2,1)} %pack_grads.1.after_ref), calls=%async_computation | async-start | bytes 819200 | tf_op jit(solution)/shard_map/all_to_all | solution.py:547
  27.2 0.8 copy-start.2
  27.9 1.0 copy-start.3
  35.0 1.3 %copy-start = (f32[264,2048]{1,0:T(8,128)}, f32[264,2048]{1,0:T(8,128)S(1)}, u32[]{:S(2)}) copy-start(f32[264,2048]{1,0:T(8,128)S(1)} %get-tuple-element.22.refs_5_) | copy-start | bytes 6488068
  36.4 3.8 %collective-permute-start.4 = (bf16[8,200,128]{2,1,0:T(8,128)(2,1)S(1)}, bf16[8,200,128]{2,1,0:T(8,128)(2,1)}, u32[]{:S(2)}, u32[]{:S(2)}) collective-permute-start(bf16[8,200,128]{2,1,0:T(8,128)(2,1)S(1)} %tie.7.refs_2_), channel_id=1, source_target_pairs={{0,1},{1,0},{2,3},{3,2},{4,5},{5,4},{6,7},{7,6},{8,9},{9,8},{10,11... | collective-permute-start | bytes 1228808 | tf_op jit(solution)/shard_map/ppermute | solution.py:543
  39.6 1.6 %copy-start.1 = (f32[264,2048]{1,0:T(8,128)S(1)}, f32[264,2048]{1,0:T(8,128)}, u32[]{:S(2)}) copy-start(f32[264,2048]{1,0:T(8,128)} %copy-done) | copy-start | bytes 6488068
  39.6 1.6 %copy-start.4 = (bf16[8,200,128]{2,1,0:T(8,128)(2,1)S(1)}, bf16[8,200,128]{2,1,0:T(8,128)(2,1)}, u32[]{:S(2)}) copy-start(bf16[8,200,128]{2,1,0:T(8,128)(2,1)} %copy-done.2) | copy-start | bytes 1228804
  39.6 10.5 %collective-permute-start.2 = (bf16[8,200,128]{2,1,0:T(8,128)(2,1)S(1)}, bf16[8,200,128]{2,1,0:T(8,128)(2,1)S(1)}, u32[]{:S(2)}, u32[]{:S(2)}) collective-permute-start(bf16[8,200,128]{2,1,0:T(8,128)(2,1)S(1)} %tie.6.refs_0_), channel_id=1, source_target_pairs={{0,2},{1,3},{2,0},{3,1},{4,6},{5,7},{6,4},{7,5},{8,10},{9,11},{10,... | collective-permute-start | bytes 1228808 | tf_op jit(solution)/shard_map/ppermute | solution.py:543
  40.1 10.0 %collective-permute-start.1 = (bf16[8,200,128]{2,1,0:T(8,128)(2,1)S(1)}, bf16[8,200,128]{2,1,0:T(8,128)(2,1)S(1)}, u32[]{:S(2)}, u32[]{:S(2)}) collective-permute-start(bf16[8,200,128]{2,1,0:T(8,128)(2,1)S(1)} %tie.6.refs_0_), channel_id=1, source_target_pairs={{0,1},{1,0},{2,3},{3,2},{4,5},{5,4},{6,7},{7,6},{8,9},{9,8},{10,11... | collective-permute-start | bytes 1228808 | tf_op jit(solution)/shard_map/ppermute | solution.py:543
  49.2 5.9 %copy-start.6 = (bf16[264,2048]{1,0:T(8,128)(2,1)}, bf16[264,2048]{1,0:T(8,128)(2,1)S(1)}, u32[]{:S(2)}) copy-start(bf16[264,2048]{1,0:T(8,128)(2,1)S(1)} %get-tuple-element.36.left_ref) | copy-start | bytes 3244036
  50.1 5.1 %collective-permute-start.5 = (bf16[8,200,128]{2,1,0:T(8,128)(2,1)S(1)}, bf16[8,200,128]{2,1,0:T(8,128)(2,1)S(1)}, u32[]{:S(2)}, u32[]{:S(2)}) collective-permute-start(bf16[8,200,128]{2,1,0:T(8,128)(2,1)S(1)} %tie.8.refs_2_), channel_id=1, source_target_pairs={{0,1},{1,0},{2,3},{3,2},{4,5},{5,4},{6,7},{7,6},{8,9},{9,8},{10,11... | collective-permute-start | bytes 1228808 | tf_op jit(solution)/shard_map/ppermute | solution.py:543
  69.0 1.9 %collective-permute-start.7 = (bf16[8,200,128]{2,1,0:T(8,128)(2,1)S(1)}, bf16[8,200,128]{2,1,0:T(8,128)(2,1)S(1)}, u32[]{:S(2)}, u32[]{:S(2)}) collective-permute-start(bf16[8,200,128]{2,1,0:T(8,128)(2,1)S(1)} %get-tuple-element.30), channel_id=1, source_target_pairs={{0,1},{1,0},{2,3},{3,2},{4,5},{5,4},{6,7},{7,6},{8,9},{9,8},{10,11... | collective-permute-start | bytes 1228808 | tf_op jit(solution)/shard_map/ppermute | solution.py:543
  69.5 18.4 %collective-permute-start.6 = (bf16[8,200,128]{2,1,0:T(8,128)(2,1)S(1)}, bf16[8,200,128]{2,1,0:T(8,128)(2,1)S(1)}, u32[]{:S(2)}, u32[]{:S(2)}) collective-permute-start(bf16[8,200,128]{2,1,0:T(8,128)(2,1)S(1)} %get-tuple-element.28), channel_id=1, source_target_pairs={{0,1},{1,0},{2,3},{3,2},{4,5},{5,4},{6,7},{7,6},{8,9},{9,8},{10,11... | collective-permute-start | bytes 1228808 | tf_op jit(solution)/shard_map/ppermute | solution.py:543
  71.0 16.9 %collective-permute-start.8 = (bf16[8,200,128]{2,1,0:T(8,128)(2,1)S(1)}, bf16[8,200,128]{2,1,0:T(8,128)(2,1)S(1)}, u32[]{:S(2)}, u32[]{:S(2)}) collective-permute-start(bf16[8,200,128]{2,1,0:T(8,128)(2,1)S(1)} %add_convert_fusion.1), channel_id=1, source_target_pairs={{0,2},{1,3},{2,0},{3,1},{4,6},{5,7},{6,4},{7,5},{8,10},{9,11},{10,... | collective-permute-start | bytes 1228808 | tf_op jit(solution)/shard_map/ppermute | solution.py:543
  88.8 16.8 %all-to-all-start.2 = ((bf16[8,200,128]{2,1,0:T(8,128)(2,1)}), bf16[8,200,128]{2,1,0:T(8,128)(2,1)S(1)}, u32[]{:S(2)}, u32[]{:S(2)}) async-start(bf16[8,200,128]{2,1,0:T(8,128)(2,1)} %add_convert_fusion), calls=%async_computation.2 | async-start | bytes 819200 | tf_op jit(solution)/shard_map/all_to_all | solution.py:547
  93.3 12.3 %copy-start.5 = (s32[128,2]{0,1:T(2,128)S(1)}, s32[128,2]{0,1:T(2,128)}, u32[]{:S(2)}) copy-start(s32[128,2]{0,1:T(2,128)} %param.9) | copy-start | bytes 3076
